TPU v7x, 32 devices: a whole 2x2x4 slice. The times are simulated.
32 devices in a mesh: dp: 8 (over z, y), mp: 4 (over x, core).
Axes of the slice: x: 2, y: 2, z: 4, core: 2. Of those that a mesh axis runs over, the one named last changes fastest.
Arguments:
- block_in: float32 [4096, 1152], P('dp'), may hold values from -6 to 6
- out_grad: float32 [4096, 1152], P('dp'), may hold values from -6 to 6
- segment_ids: int32 [4096], replicated, may hold values from 0 to 3, never falling along the last dimension, each value on 1 to 2048 neighbouring positions
- w_query: float32 [1152, 1024], P('dp', 'mp'), may hold values from -0.1875 to 0.1875
- w_keyval: float32 [1152, 512], P(('dp', 'mp')), may hold values from -0.1875 to 0.1875
- w_out: float32 [1024, 1152], P('mp', 'dp'), may hold values from -0.1875 to 0.1875
- w_gateup: float32 [2, 1152, 6912], P(None, 'dp', 'mp'), may hold values from -0.1875 to 0.1875
- w_down: float32 [6912, 1152], P('mp', 'dp'), may hold values from -0.078125 to 0.078125
- gain_layers: float32 [4, 1152], P(None, ('dp', 'mp')), may hold values from -0.04 to 0.04
- gain_heads: float32 [2, 256], P(None, ('dp', 'mp')), may hold values from -0.04 to 0.04
- mom_query: float32 [1152, 1024], P('dp', 'mp'), may hold values from -0.18 to 0.18
- var_query: float32 [1152, 1024], P('dp', 'mp'), may hold values from 0.025 to 0.1
- mom_keyval: float32 [1152, 512], P(('dp', 'mp')), may hold values from -0.18 to 0.18
- var_keyval: float32 [1152, 512], P(('dp', 'mp')), may hold values from 0.02 to 4
- mom_out: float32 [1024, 1152], P('mp', 'dp'), may hold values from -0.18 to 0.18
- var_out: float32 [1024, 1152], P('mp', 'dp'), may hold values from 0.025 to 0.1
- mom_gateup: float32 [2, 1152, 6912], P(None, 'dp', 'mp'), may hold values from -0.18 to 0.18
- var_gateup: float32 [2, 1152, 6912], P(None, 'dp', 'mp'), may hold values from 0.025 to 0.1
- mom_down: float32 [6912, 1152], P('mp', 'dp'), may hold values from -0.18 to 0.18
- var_down: float32 [6912, 1152], P('mp', 'dp'), may hold values from 0.025 to 0.1
- mom_layers: float32 [4, 1152], P(None, ('dp', 'mp')), may hold values from -0.18 to 0.18
- var_layers: float32 [4, 1152], P(None, ('dp', 'mp')), may hold values from 0.025 to 0.1
- mom_heads: float32 [2, 256], P(None, ('dp', 'mp')), may hold values from -0.18 to 0.18
- var_heads: float32 [2, 256], P(None, ('dp', 'mp')), may hold values from 0.02 to 4
Outputs:
- block_out: float32 [4096, 1152], P('dp')
- grad_input: float32 [4096, 1152], P('dp')
- grad_query: float32 [1152, 1024], P('dp', 'mp')
- grad_keyval: float32 [1152, 512], P(('dp', 'mp'))
- grad_out: float32 [1024, 1152], P('mp', 'dp')
- grad_gateup: float32 [2, 1152, 6912], P(None, 'dp', 'mp')
- grad_down: float32 [6912, 1152], P('mp', 'dp')
- grad_layers: float32 [4, 1152], P(None, ('dp', 'mp'))
- grad_heads: float32 [2, 256], P(None, ('dp', 'mp'))
- fresh_query: float32 [1152, 1024], P('dp', 'mp')
- fresh_keyval: float32 [1152, 512], P(('dp', 'mp'))
- fresh_out: float32 [1024, 1152], P('mp', 'dp')
- fresh_gateup: float32 [2, 1152, 6912], P(None, 'dp', 'mp')
- fresh_down: float32 [6912, 1152], P('mp', 'dp')
- fresh_layers: float32 [4, 1152], P(None, ('dp', 'mp'))
- fresh_heads: float32 [2, 256], P(None, ('dp', 'mp'))
- fresh_mom_query: float32 [1152, 1024], P('dp', 'mp')
- fresh_mom_keyval: float32 [1152, 512], P(('dp', 'mp'))
- fresh_mom_out: float32 [1024, 1152], P('mp', 'dp')
- fresh_mom_gateup: float32 [2, 1152, 6912], P(None, 'dp', 'mp')
- fresh_mom_down: float32 [6912, 1152], P('mp', 'dp')
- fresh_mom_layers: float32 [4, 1152], P(None, ('dp', 'mp'))
- fresh_mom_heads: float32 [2, 256], P(None, ('dp', 'mp'))
- fresh_var_query: float32 [1152, 1024], P('dp', 'mp')
- fresh_var_keyval: float32 [1152, 512], P(('dp', 'mp'))
- fresh_var_out: float32 [1024, 1152], P('mp', 'dp')
- fresh_var_gateup: float32 [2, 1152, 6912], P(None, 'dp', 'mp')
- fresh_var_down: float32 [6912, 1152], P('mp', 'dp')
- fresh_var_layers: float32 [4, 1152], P(None, ('dp', 'mp'))
- fresh_var_heads: float32 [2, 256], P(None, ('dp', 'mp'))
Inputs may be any that keep to these rules, and one draw needn't show every extreme that they name: `segment_ids`: document ids, never falling along the tokens; a document has 2048 tokens or fewer.
All inputs are finite; a program needn't handle non-finite values.
Results may differ from a plain program's by a relative error of at most 0.025.
Values may be sent and summed in bfloat16 or wider, within the bound.
No kernel may reach another device: no remote copies, remote signals or barrier semaphores. Data moves between devices by JAX's collectives and lax.ppermute only.
A program may use at most 192 MiB of HBM per device.

v0:
```python
import jax
import jax.numpy as jnp
from jax import lax
from jax.sharding import PartitionSpec as P

HD = 256
SEQ = 2048
ADAM_STEP = 4


EPS = 1e-06
THETA = 1000000.0
LEARN = 0.02
BETA_ONE = 0.9
BETA_TWO = 0.95
ADAM_EPS = 1e-08
DECAY = 0.1
GELU_COEF = 0.7978845608028654
GELU_CUBE = 0.044715
NEG_FILL = -1e30


def shifted(value, axis, by):
    length = lax.axis_size(axis)
    pairs = [(i, i + by) for i in range(length) if 0 <= i + by < length]
    return lax.ppermute(value, axis, pairs)


def rms_scale(values):
    return lax.rsqrt(jnp.mean(values * values, axis=-1, keepdims=True) + EPS)


def norm_back(values, scale, factor, incoming):
    scaled = incoming * factor
    return scale * (
        scaled - values * (scale * scale) * jnp.mean(scaled * values, axis=-1, keepdims=True)
    )


def rotate_half(values):
    middle = values.shape[-1] // 2
    return jnp.concatenate([-values[..., middle:], values[..., :middle]], axis=-1)


def rope_tables(position, width):
    middle = width // 2
    freqs = THETA ** (-2.0 * jnp.arange(middle, dtype=jnp.float32) / width)
    angle = position.astype(jnp.float32)[:, None] * freqs[None, :]
    cosine = jnp.concatenate([jnp.cos(angle), jnp.cos(angle)], axis=-1)
    sine = jnp.concatenate([jnp.sin(angle), jnp.sin(angle)], axis=-1)
    return (cosine, sine)


def gelu_parts(values):
    inner = GELU_COEF * (values + GELU_CUBE * values * values * values)
    tanh_val = jnp.tanh(inner)
    value = 0.5 * values * (1.0 + tanh_val)
    slope = 0.5 * (1.0 + tanh_val) + 0.5 * values * (1.0 - tanh_val * tanh_val) * GELU_COEF * (
        1.0 + 3.0 * GELU_CUBE * values * values
    )
    return (value, slope)


def adam_update(weight, mom, var, grad, decay):
    mom_new = BETA_ONE * mom + (1.0 - BETA_ONE) * grad
    var_new = BETA_TWO * var + (1.0 - BETA_TWO) * grad * grad
    fix_one = 1.0 - BETA_ONE**ADAM_STEP
    fix_two = 1.0 - BETA_TWO**ADAM_STEP
    direction = mom_new / fix_one / (jnp.sqrt(var_new / fix_two) + ADAM_EPS)
    return (weight - LEARN * (direction + decay * weight), mom_new, var_new)


def reduce_model(local_sum):
    return lax.psum(local_sum, "mp")


def on_device(
    block_in,
    out_grad,
    segment_ids,
    w_query,
    w_keyval,
    w_out,
    w_gateup,
    w_down,
    gain_layers,
    gain_heads,
    mom_query,
    var_query,
    mom_keyval,
    var_keyval,
    mom_out,
    var_out,
    mom_gateup,
    var_gateup,
    mom_down,
    var_down,
    mom_layers,
    var_layers,
    mom_heads,
    var_heads,
):
    bf = jnp.bfloat16
    fl = jnp.float32
    low_query, low_out, low_gateup, low_down = (
        lax.all_gather(w_query.astype(bf), "dp", axis=0, tiled=True),
        lax.all_gather(w_out.astype(bf), "dp", axis=1, tiled=True),
        lax.all_gather(w_gateup.astype(bf), "dp", axis=1, tiled=True),
        lax.all_gather(w_down.astype(bf), "dp", axis=1, tiled=True),
    )
    low_keyval, low_layers, low_heads = (
        lax.all_gather(w_keyval.astype(bf), ("dp", "mp"), axis=0, tiled=True),
        lax.all_gather(gain_layers.astype(bf), ("dp", "mp"), axis=1, tiled=True),
        lax.all_gather(gain_heads.astype(bf), ("dp", "mp"), axis=1, tiled=True),
    )
    gain_scale = 1.0 + low_layers.astype(fl)
    head_scale = 1.0 + low_heads.astype(fl)
    rows = block_in.shape[0]
    width = HD
    margin = SEQ // 2
    heads = low_query.shape[1] // width
    factor = width ** (-0.5)
    norm_factor = float(rows * lax.axis_size("dp")) ** (-0.5)
    quarter = rows // lax.axis_size("mp")
    offset = lax.axis_index("mp") * quarter
    device = lax.axis_index("dp")
    first_row = device * rows
    shifted_first = first_row + margin
    seq_start = shifted_first // SEQ * SEQ
    own_place = shifted_first - seq_start
    span_count = SEQ // rows
    position = shifted_first + jnp.arange(rows, dtype=jnp.int32)
    cosine, sine = rope_tables(position % SEQ, width)

    def part_rows(values):
        return lax.dynamic_slice_in_dim(values, offset, quarter, 0)

    scale_in = rms_scale(block_in)
    normed_in = (block_in * scale_in * gain_scale[0]).astype(bf)
    query_raw = jnp.dot(normed_in, low_query, preferred_element_type=fl).reshape(rows, heads, width)
    keyval_raw = jnp.dot(normed_in, low_keyval, preferred_element_type=fl)
    key_raw = keyval_raw[:, :width]
    scale_key = rms_scale(key_raw)
    key_norm = key_raw * scale_key * head_scale[1]
    key_rot = key_norm * cosine + rotate_half(key_norm) * sine
    keyval_low = jnp.concatenate([key_rot, keyval_raw[:, width:]], axis=1).astype(bf)
    start_keyval = lax.dynamic_update_slice_in_dim(
        jnp.zeros((SEQ, 2 * width), bf), keyval_low, own_place, 0
    )

    def collect(turn, state):
        moving, collected = state
        moving = shifted(moving, "dp", 1)
        target = own_place - (turn + 1) * rows
        placed = lax.dynamic_update_slice_in_dim(collected, moving, jnp.maximum(target, 0), 0)
        return (moving, jnp.where(target >= 0, placed, collected))

    seq_keyval = lax.fori_loop(0, span_count - 1, collect, (keyval_low, start_keyval))[1]
    scale_query = rms_scale(query_raw)
    query_norm = query_raw * scale_query * head_scale[0]
    query_rot = (
        query_norm * cosine[:, None, :] + rotate_half(query_norm) * sine[:, None, :]
    ).astype(bf)
    seq_keys = seq_keyval[:, :width]
    seq_values = seq_keyval[:, width:]
    padded_seg = jnp.pad(segment_ids, (margin, margin), constant_values=-1)
    seg_query = lax.dynamic_slice_in_dim(segment_ids, first_row, rows, 0)
    seg_keys = lax.dynamic_slice_in_dim(padded_seg, seq_start, SEQ, 0)
    key_index = seq_start + jnp.arange(SEQ, dtype=jnp.int32)
    allowed = (key_index[None, :] <= position[:, None]) & (seg_keys[None, :] == seg_query[:, None])
    scores = jnp.einsum("qhd,kd->hqk", query_rot, seq_keys, preferred_element_type=fl) * factor
    masked = jnp.where(allowed[None], scores, NEG_FILL)
    top = jnp.max(masked, axis=-1, keepdims=True)
    log_total = top + jnp.log(jnp.sum(jnp.exp(masked - top), axis=-1, keepdims=True))
    probs = jnp.exp(masked - log_total)
    probs_low = probs.astype(bf)
    attended3 = jnp.einsum("hqk,kd->qhd", probs_low, seq_values, preferred_element_type=fl).astype(
        bf
    )
    attended = attended3.reshape(rows, heads * width)
    attn_proj = reduce_model(jnp.dot(attended, low_out, preferred_element_type=fl))
    scale_attn = rms_scale(attn_proj)
    resid = block_in + attn_proj * scale_attn * gain_scale[1]
    scale_mid = rms_scale(resid)
    normed_mid = (resid * scale_mid * gain_scale[2]).astype(bf)
    gate_raw = jnp.dot(normed_mid, low_gateup[0], preferred_element_type=fl)
    up_raw = jnp.dot(normed_mid, low_gateup[1], preferred_element_type=fl)
    gelu_value, gelu_slope = gelu_parts(gate_raw)
    hidden = (gelu_value * up_raw).astype(bf)
    ffn_proj = reduce_model(jnp.dot(hidden, low_down, preferred_element_type=fl))
    scale_ffn = rms_scale(ffn_proj)
    block_out = resid + ffn_proj * scale_ffn * gain_scale[3]
    grad_ffn = norm_back(ffn_proj, scale_ffn, gain_scale[3], out_grad).astype(bf)
    grad_down = jnp.einsum("tf,td->fd", hidden, grad_ffn, preferred_element_type=fl)
    grad_hidden = jnp.einsum("td,fd->tf", grad_ffn, low_down, preferred_element_type=fl)
    grad_gate = (grad_hidden * up_raw * gelu_slope).astype(bf)
    grad_up = (grad_hidden * gelu_value).astype(bf)
    grad_gateup = jnp.stack(
        [
            jnp.einsum("td,tf->df", normed_mid, grad_gate, preferred_element_type=fl),
            jnp.einsum("td,tf->df", normed_mid, grad_up, preferred_element_type=fl),
        ]
    )
    grad_mid = reduce_model(
        jnp.einsum("tf,df->td", grad_gate, low_gateup[0], preferred_element_type=fl)
        + jnp.einsum("tf,df->td", grad_up, low_gateup[1], preferred_element_type=fl)
    )
    grad_resid = out_grad + norm_back(resid, scale_mid, gain_scale[2], grad_mid)
    grad_attn = norm_back(attn_proj, scale_attn, gain_scale[1], grad_resid).astype(bf)
    grad_out = jnp.einsum("tc,td->cd", attended, grad_attn, preferred_element_type=fl)
    grad_attended = (
        jnp.einsum("td,cd->tc", grad_attn, low_out, preferred_element_type=fl)
        .astype(bf)
        .reshape(rows, heads, width)
    )
    row_delta = jnp.sum(grad_attended.astype(fl) * attended3.astype(fl), axis=-1)
    grad_probs = jnp.einsum("qhd,kd->hqk", grad_attended, seq_values, preferred_element_type=fl)
    grad_scores = (probs * (grad_probs - row_delta.T[:, :, None]) * factor).astype(bf)
    grad_qrot = jnp.einsum("hqk,kd->qhd", grad_scores, seq_keys, preferred_element_type=fl)
    grad_krot_seq = jnp.einsum("hqk,qhd->kd", grad_scores, query_rot, preferred_element_type=fl)
    grad_values_seq = jnp.einsum("hqk,qhd->kd", probs_low, grad_attended, preferred_element_type=fl)
    grad_seq = jnp.concatenate([grad_krot_seq, grad_values_seq], axis=1)

    def block_for(back):
        target = (device - back) * rows + margin - seq_start
        picked = lax.dynamic_slice_in_dim(grad_seq, jnp.maximum(target, 0), rows, 0)
        return jnp.where(target >= 0, picked, 0.0)

    def carry_on(turn, running):
        moved = shifted(running.astype(jnp.bfloat16), "dp", -1).astype(running.dtype)
        return moved + block_for(span_count - 2 - turn)

    grad_own = lax.fori_loop(0, span_count - 1, carry_on, block_for(span_count - 1))
    grad_kpart = lax.psum_scatter(
        grad_own.astype(jnp.bfloat16), "mp", scatter_dimension=0, tiled=True
    ).astype(jnp.float32)
    cos_part = part_rows(cosine)
    sin_part = part_rows(sine)
    key_part = part_rows(key_raw)
    scale_kpart = part_rows(scale_key)
    grad_krot = grad_kpart[:, :width]
    key_back = grad_krot * cos_part - rotate_half(grad_krot * sin_part)
    grad_kin = norm_back(key_part, scale_kpart, head_scale[1], key_back)
    grad_kvin = jnp.concatenate([grad_kin, grad_kpart[:, width:]], axis=1).astype(bf)
    grad_keyval = jnp.einsum(
        "td,tc->dc", part_rows(normed_in), grad_kvin, preferred_element_type=fl
    )
    query_back = grad_qrot * cosine[:, None, :] - rotate_half(grad_qrot * sine[:, None, :])
    grad_qin = (
        norm_back(query_raw, scale_query, head_scale[0], query_back)
        .astype(bf)
        .reshape(rows, heads * width)
    )
    grad_query = jnp.einsum("td,tc->dc", normed_in, grad_qin, preferred_element_type=fl)
    normed_part = jnp.einsum("tc,dc->td", grad_qin, low_query, preferred_element_type=fl)
    keyval_part = jnp.einsum("tc,dc->td", grad_kvin, low_keyval, preferred_element_type=fl)
    normed_part = lax.dynamic_update_slice_in_dim(
        normed_part, part_rows(normed_part) + keyval_part, offset, 0
    )
    grad_normed = reduce_model(normed_part)
    grad_input = grad_resid + norm_back(block_in, scale_in, gain_scale[0], grad_normed)
    grad_layers = jnp.stack(
        [
            jnp.sum(part_rows(grad_normed) * part_rows(block_in) * part_rows(scale_in), axis=0),
            jnp.sum(part_rows(grad_resid) * part_rows(attn_proj) * part_rows(scale_attn), axis=0),
            jnp.sum(part_rows(grad_mid) * part_rows(resid) * part_rows(scale_mid), axis=0),
            jnp.sum(part_rows(out_grad) * part_rows(ffn_proj) * part_rows(scale_ffn), axis=0),
        ]
    )
    grad_heads = jnp.stack(
        [
            jnp.sum(query_back * query_raw * scale_query, axis=(0, 1)),
            jnp.sum(key_back * key_part * scale_kpart, axis=0),
        ]
    )
    sum_query, sum_out, sum_gateup, sum_down = (
        lax.psum_scatter(
            grad_query.astype(jnp.bfloat16), "dp", scatter_dimension=0, tiled=True
        ).astype(jnp.float32),
        lax.psum_scatter(
            grad_out.astype(jnp.bfloat16), "dp", scatter_dimension=1, tiled=True
        ).astype(jnp.float32),
        lax.psum_scatter(
            grad_gateup.astype(jnp.bfloat16), "dp", scatter_dimension=1, tiled=True
        ).astype(jnp.float32),
        lax.psum_scatter(
            grad_down.astype(jnp.bfloat16), "dp", scatter_dimension=1, tiled=True
        ).astype(jnp.float32),
    )
    sum_keyval, sum_layers, sum_heads = (
        lax.psum_scatter(grad_keyval, ("dp", "mp"), scatter_dimension=0, tiled=True),
        lax.psum_scatter(grad_layers, ("dp", "mp"), scatter_dimension=1, tiled=True),
        lax.psum_scatter(grad_heads, ("dp", "mp"), scatter_dimension=1, tiled=True),
    )
    masters = (w_query, w_keyval, w_out, w_gateup, w_down, gain_layers, gain_heads)
    sums = (sum_query, sum_keyval, sum_out, sum_gateup, sum_down, sum_layers, sum_heads)
    totals = tuple((item * norm_factor for item in sums))
    moms = (mom_query, mom_keyval, mom_out, mom_gateup, mom_down, mom_layers, mom_heads)
    varis = (var_query, var_keyval, var_out, var_gateup, var_down, var_layers, var_heads)
    decays = (DECAY, DECAY, DECAY, DECAY, DECAY, 0.0, 0.0)
    updated = [
        adam_update(master, mom, var, grad, decay)
        for master, mom, var, grad, decay in zip(masters, moms, varis, totals, decays)
    ]
    fresh = tuple((item[0] for item in updated))
    fresh_moms = tuple((item[1] for item in updated))
    fresh_vars = tuple((item[2] for item in updated))
    return (
        block_out,
        grad_input,
        totals[0],
        totals[1],
        totals[2],
        totals[3],
        totals[4],
        totals[5],
        totals[6],
        fresh[0],
        fresh[1],
        fresh[2],
        fresh[3],
        fresh[4],
        fresh[5],
        fresh[6],
        fresh_moms[0],
        fresh_moms[1],
        fresh_moms[2],
        fresh_moms[3],
        fresh_moms[4],
        fresh_moms[5],
        fresh_moms[6],
        fresh_vars[0],
        fresh_vars[1],
        fresh_vars[2],
        fresh_vars[3],
        fresh_vars[4],
        fresh_vars[5],
        fresh_vars[6],
    )


def solution(mesh):
    in_specs = (
        P("dp", None),
        P("dp", None),
        P(),
        P("dp", "mp"),
        P(("dp", "mp"), None),
        P("mp", "dp"),
        P(None, "dp", "mp"),
        P("mp", "dp"),
        P(None, ("dp", "mp")),
        P(None, ("dp", "mp")),
        P("dp", "mp"),
        P("dp", "mp"),
        P(("dp", "mp"), None),
        P(("dp", "mp"), None),
        P("mp", "dp"),
        P("mp", "dp"),
        P(None, "dp", "mp"),
        P(None, "dp", "mp"),
        P("mp", "dp"),
        P("mp", "dp"),
        P(None, ("dp", "mp")),
        P(None, ("dp", "mp")),
        P(None, ("dp", "mp")),
        P(None, ("dp", "mp")),
    )
    out_specs = (
        P("dp", None),
        P("dp", None),
        P("dp", "mp"),
        P(("dp", "mp"), None),
        P("mp", "dp"),
        P(None, "dp", "mp"),
        P("mp", "dp"),
        P(None, ("dp", "mp")),
        P(None, ("dp", "mp")),
        P("dp", "mp"),
        P(("dp", "mp"), None),
        P("mp", "dp"),
        P(None, "dp", "mp"),
        P("mp", "dp"),
        P(None, ("dp", "mp")),
        P(None, ("dp", "mp")),
        P("dp", "mp"),
        P(("dp", "mp"), None),
        P("mp", "dp"),
        P(None, "dp", "mp"),
        P("mp", "dp"),
        P(None, ("dp", "mp")),
        P(None, ("dp", "mp")),
        P("dp", "mp"),
        P(("dp", "mp"), None),
        P("mp", "dp"),
        P(None, "dp", "mp"),
        P("mp", "dp"),
        P(None, ("dp", "mp")),
        P(None, ("dp", "mp")),
    )
    return jax.shard_map(
        on_device, mesh=mesh, in_specs=in_specs, out_specs=out_specs, check_vma=False
    )
```

profile of v0, /device:TPU:0, one launch (start us, length us, event | category | flops | bytes accessed | tf_op | source)
XLA Modules:
  0.0 1228.5 jit_solution(5174310431227354650)
XLA Ops:
  14.9 43.0 %all-gather.2 = bf16[32,8,2]{1,2,0:T(2,128)(2,1)S(1)} all-gather(bf16[1,8,2]{1,2,0:T(2,128)(2,1)S(1)} %convert_bitcast_fusion.2), channel_id=1, replica_groups=mesh['dp'=8,'mp'=4] {'dp','mp'}, dimensions={0}, use_global_device_ids=true | all-gather | bytes 1056 | tf_op jit(solution)/shard_map/all_gather | solution.py:114
  59.4 36.6 %all-gather = bf16[32,36,4]{1,2,0:T(4,128)(2,1)S(1)} all-gather(bf16[1,36,4]{1,2,0:T(4,128)(2,1)S(1)} %convert_bitcast_fusion.1), channel_id=1, replica_groups=mesh['dp'=8,'mp'=4] {'dp','mp'}, dimensions={0}, use_global_device_ids=true | all-gather | bytes 9504 | tf_op jit(solution)/shard_map/all_gather | solution.py:113
  97.5 33.5 %all_gather.24 = bf16[1152,256]{1,0:T(8,128)(2,1)} all-gather(bf16[144,256]{1,0:T(8,128)(2,1)S(1)} %convert_element_type.138), channel_id=1, replica_groups=mesh['dp'=8,'mp'=4] {'dp'}, dimensions={0}, use_global_device_ids=true | all-gather | bytes 663552 | tf_op jit(solution)/shard_map/all_gather | solution.py:106
  135.8 33.6 %all_gather.25 = bf16[256,1152]{0,1:T(8,128)(2,1)} all-gather(bf16[256,144]{0,1:T(8,128)(2,1)S(1)} %copy-done.51), channel_id=1, replica_groups=mesh['dp'=8,'mp'=4] {'dp'}, dimensions={1}, use_global_device_ids=true | all-gather | bytes 663552 | tf_op jit(solution)/shard_map/all_gather | solution.py:107
  174.4 50.2 %while.28 = (s32[]{:T(128)}, bf16[512,512]{1,0:T(8,128)(2,1)S(1)}, bf16[2048,512]{1,0:T(8,128)(2,1)S(1)}, s32[]{:T(128)}, s32[]{:T(128)}, /*index=5*/s32[]{:T(128)}, s32[]{:T(128)}) while((s32[]{:T(128)}, bf16[512,512]{1,0:T(8,128)(2,1)S(1)}, bf16[2048,512]{1,0:T(8,128)(2,1)S(1)}, s32[]{:T(128)}, s32[]{:T(128)}, /*index=5*/s32[]{:T(128)}, ...), condition=%wide.region_3.4_spmd, body=%wide.region_2.3_spmd.sunk | while | flops 262150 | bytes 5767339 | solution.py:158
  175.7 11.9 collective-permute-done
  195.4 11.4 collective-permute-done
  233.7 54.2 %all-reduce.13.cloned.1.call-done = f32[512,1152]{1,0:T(8,128)} async-done(((f32[512,1152]{1,0:T(8,128)}), f32[512,1152]{1,0:T(8,128)}) %all-reduce.13.cloned.1.call-update) | async-done | bytes 2359312 | tf_op jit(solution)/shard_map/psum | solution.py:74
  294.2 64.1 %all-gather.7.cloned.1.call-done = bf16[2,1152,1728]{2,1,0:T(8,128)(2,1)} async-done(((bf16[2,144,1728]{2,1,0:T(8,128)(2,1)}), bf16[2,1152,1728]{2,1,0:T(8,128)(2,1)}) %all-gather.7.cloned.1.call-update) | async-done | bytes 7962640 | tf_op jit(solution)/shard_map/all_gather | solution.py:108
  370.3 61.0 %all-gather.9.cloned.1.call-done = bf16[1728,1152]{0,1:T(8,128)(2,1)} async-done(((bf16[1728,144]{0,1:T(8,128)(2,1)}), bf16[1728,1152]{0,1:T(8,128)(2,1)}) %all-gather.9.cloned.1.call-update) | async-done | bytes 3981328 | tf_op jit(solution)/shard_map/all_gather | solution.py:109
  438.2 54.0 %all-reduce.15.cloned.1.call-done = f32[512,1152]{1,0:T(8,128)} async-done(((f32[512,1152]{1,0:T(8,128)}), f32[512,1152]{1,0:T(8,128)}) %all-reduce.15.cloned.1.call-update) | async-done | bytes 2359312 | tf_op jit(solution)/shard_map/psum | solution.py:74
  499.1 8.1 multiply_convert_fusion
  514.4 55.5 %all-reduce.17.cloned.1.call-done = f32[512,1152]{1,0:T(8,128)} async-done(((f32[512,1152]{1,0:T(8,128)}), f32[512,1152]{1,0:T(8,128)}) %all-reduce.17.cloned.1.call-update) | async-done | bytes 2359312 | tf_op jit(solution)/shard_map/psum | solution.py:74
  587.7 48.7 %while.29 = (s32[]{:T(128)}, bf16[512,512]{1,0:T(8,128)(2,1)}, s32[]{:T(128)}, s32[]{:T(128)}, f32[2048,512]{0,1:T(8,128)}, /*index=5*/s32[]{:T(128)}, s32[]{:T(128)}, s32[]{:T(128)}, s32[]{:T(128)}, s32[]{:T(128)}) while((s32[]{:T(128)}, bf16[512,512]{1,0:T(8,128)(2,1)}, s32[]{:T(128)}, s32[]{:T(128)}, f32[2048,512]{0,1:T(8,128)}, ...), condition=%wide.region_19.20_spmd, body=%wide.region_18.19_spmd.sunk | while | flops 1048585 | bytes 8388835 | solution.py:233
  591.0 12.4 %collective-permute-done.1 = bf16[512,512]{1,0:T(8,128)(2,1)S(1)} collective-permute-done((bf16[512,512]{1,0:T(8,128)(2,1)}, bf16[512,512]{1,0:T(8,128)(2,1)S(1)}, u32[]{:S(2)}, u32[]{:S(2)}) %collective-permute-start.1) | collective-permute-done | bytes 524320 | tf_op jit(solution)/shard_map/while/body/eval_jaxpr/ppermute | solution.py:26
  607.7 12.1 collective-permute-done.1
  624.1 11.5 collective-permute-done.1
  681.1 22.9 %copy.106 = bf16[2,1152,1728]{2,0,1:T(2,128)(2,1)} copy(bf16[2,1152,1728]{1,2,0:T(8,128)(2,1)} %pad_maximum_fusion) | data formatting | bytes 15925248 | tf_op jit(solution)/shard_map/stack | solution.py:198
  721.1 84.0 %fusion = f32[40,512]{1,0:T(8,128)S(1)} fusion(f32[1152,512]{1,0:T(8,128)} %fusion.56), kind=kCustom, calls=%all-reduce-scatter | all-reduce-scatter fusion | flops 655361 | bytes 2441216
  823.0 31.7 %all-reduce.19.cloned.1.call-done = f32[512,1152]{1,0:T(8,128)} async-done(((f32[512,1152]{1,0:T(8,128)}), f32[512,1152]{1,0:T(8,128)}) %all-reduce.19.cloned.1.call-update) | async-done | bytes 2359312 | tf_op jit(solution)/shard_map/psum | solution.py:74
  855.9 43.1 %all-reduce.6 = (f32[4,1152]{1,0:T(4,128)S(1)}, f32[2,256]{1,0:T(2,128)S(1)}) all-reduce(f32[4,1152]{1,0:T(4,128)S(1)} %pad_maximum_fusion.8, f32[2,256]{1,0:T(2,128)S(1)} %copy-done.73), channel_id=8, replica_groups=mesh['dp'=8,'mp'=4] {'dp','mp'}, use_global_device_ids=true, to_apply=%region_33.34.clone | all-reduce | flops 5120 | bytes 40960
  904.8 221.3 %all-reduce.21.cloned.1.call-done = bf16[2,1152,1728]{2,0,1:T(2,128)(2,1)} async-done(((bf16[2,1152,1728]{2,0,1:T(2,128)(2,1)}), bf16[2,1152,1728]{2,0,1:T(2,128)(2,1)}) %all-reduce.21.cloned.1.call-update) | async-done | bytes 7962640
  1128.1 6.9 multiply_subtract_fusion
  1135.0 81.3 %reduce-scatter.15.cloned.1.call-done = bf16[1728,144]{0,1:T(8,128)(2,1)} async-done(((bf16[1728,1152]{0,1:T(8,128)(2,1)}), bf16[1728,144]{0,1:T(8,128)(2,1)}) %reduce-scatter.15.cloned.1.call-update) | async-done | bytes 497680 | tf_op jit(solution)/shard_map/reduce_scatter | solution.py:286
  (374 shorter events, 215.8 us)
Async XLA Ops:
  8.1 161.3 %all-gather.11.cloned.1.call-start = ((), (), s32[]{:S(2)}) async-start(), calls=%async_computation.13 | async-start | bytes 1351680 | tf_op jit(solution)/shard_map/all_gather | solution.py:112
  9.8 278.1 %all-reduce.13.cloned.1.call-start = ((), (), s32[]{:S(2)}) async-start(), calls=%async_computation.4 | async-start | bytes 4718592 | tf_op jit(solution)/shard_map/psum | solution.py:74
  174.4 13.3 %collective-permute-start = (bf16[512,512]{1,0:T(8,128)(2,1)S(1)}, bf16[512,512]{1,0:T(8,128)(2,1)S(1)}, u32[]{:S(2)}, u32[]{:S(2)}) collective-permute-start(bf16[512,512]{1,0:T(8,128)(2,1)S(1)} %get-tuple-element.507), channel_id=1, source_target_pairs={{0,4},{4,8},{8,12},{12,16},{16,20},{20,24},{24,28},{1,5},{5,9},{9,... | collective-permute-start | bytes 1572872 | tf_op jit(solution)/shard_map/while/body/eval_jaxpr/ppermute | solution.py:26
  191.0 15.9 %collective-permute-start = (bf16[512,512]{1,0:T(8,128)(2,1)S(1)}, bf16[512,512]{1,0:T(8,128)(2,1)S(1)}, u32[]{:S(2)}, u32[]{:S(2)}) collective-permute-start(bf16[512,512]{1,0:T(8,128)(2,1)S(1)} %get-tuple-element.507), channel_id=1, source_target_pairs={{0,4},{4,8},{8,12},{12,16},{16,20},{20,24},{24,28},{1,5},{5,9},{9,... | collective-permute-start | bytes 1572872 | tf_op jit(solution)/shard_map/while/body/eval_jaxpr/ppermute | solution.py:26
  210.2 11.1 collective-permute-start
  229.8 128.5 %all-gather.7.cloned.1.call-start = ((), (), s32[]{:S(2)}) async-start(), calls=%async_computation.5 | async-start | bytes 9289728 | tf_op jit(solution)/shard_map/all_gather | solution.py:108
  231.0 200.3 %all-gather.9.cloned.1.call-start = ((), (), s32[]{:S(2)}) async-start(), calls=%async_computation.6 | async-start | bytes 4644864 | tf_op jit(solution)/shard_map/all_gather | solution.py:109
  233.1 259.1 %all-reduce.15.cloned.1.call-start = ((), (), s32[]{:S(2)}) async-start(), calls=%async_computation.7 | async-start | bytes 4718592 | tf_op jit(solution)/shard_map/psum | solution.py:74
  292.6 279.4 %copy-start.2 = (f32[512,1152]{1,0:T(8,128)}, f32[512,1152]{1,0:T(8,128)S(1)}, u32[]{:S(2)}) copy-start(f32[512,1152]{1,0:T(8,128)S(1)} %get-tuple-element.396) | copy-start | bytes 7077892
  438.0 131.9 %all-reduce.17.cloned.1.call-start = ((), (), s32[]{:S(2)}) async-start(), calls=%async_computation.8 | async-start | bytes 4718592 | tf_op jit(solution)/shard_map/psum | solution.py:74
  514.0 147.4 %reduce-scatter.17.cloned.1.call-start = ((), (), s32[]{:S(2)}) async-start(), calls=%async_computation.14 | async-start | bytes 655360
  587.7 15.7 %collective-permute-start.1 = (bf16[512,512]{1,0:T(8,128)(2,1)}, bf16[512,512]{1,0:T(8,128)(2,1)S(1)}, u32[]{:S(2)}, u32[]{:S(2)}) collective-permute-start(bf16[512,512]{1,0:T(8,128)(2,1)} %get-tuple-element.531), channel_id=1, source_target_pairs={{4,0},{8,4},{12,8},{16,12},{20,16},{24,20},{28,24},{5,1},{9,5},{13... | collective-permute-start | bytes 1572872 | tf_op jit(solution)/shard_map/while/body/eval_jaxpr/ppermute | solution.py:26
  604.4 15.4 %collective-permute-start.1 = (bf16[512,512]{1,0:T(8,128)(2,1)}, bf16[512,512]{1,0:T(8,128)(2,1)S(1)}, u32[]{:S(2)}, u32[]{:S(2)}) collective-permute-start(bf16[512,512]{1,0:T(8,128)(2,1)} %get-tuple-element.531), channel_id=1, source_target_pairs={{4,0},{8,4},{12,8},{16,12},{20,16},{24,20},{28,24},{5,1},{9,5},{13... | collective-permute-start | bytes 1572872 | tf_op jit(solution)/shard_map/while/body/eval_jaxpr/ppermute | solution.py:26
  620.7 14.8 %collective-permute-start.1 = (bf16[512,512]{1,0:T(8,128)(2,1)}, bf16[512,512]{1,0:T(8,128)(2,1)S(1)}, u32[]{:S(2)}, u32[]{:S(2)}) collective-permute-start(bf16[512,512]{1,0:T(8,128)(2,1)} %get-tuple-element.531), channel_id=1, source_target_pairs={{4,0},{8,4},{12,8},{16,12},{20,16},{24,20},{28,24},{5,1},{9,5},{13... | collective-permute-start | bytes 1572872 | tf_op jit(solution)/shard_map/while/body/eval_jaxpr/ppermute | solution.py:26
  638.8 180.5 %reduce-scatter.13.cloned.1.call-start = ((), (), s32[]{:S(2)}) async-start(), calls=%async_computation.11 | async-start | bytes 663552 | tf_op jit(solution)/shard_map/reduce_scatter | solution.py:280
  648.2 172.8 %reduce-scatter.11.cloned.1.call-start = ((), (), s32[]{:S(2)}) async-start(), calls=%async_computation.10 | async-start | bytes 663552 | tf_op jit(solution)/shard_map/reduce_scatter | solution.py:277
  655.5 199.2 %all-reduce.19.cloned.1.call-start = ((), (), s32[]{:S(2)}) async-start(), calls=%async_computation.9 | async-start | bytes 4718592 | tf_op jit(solution)/shard_map/psum | solution.py:74
  667.7 458.4 %all-reduce.21.cloned.1.call-start = ((), (), s32[]{:S(2)}) async-start(), calls=%async_computation.15 | async-start | bytes 16515072
  704.0 512.2 %reduce-scatter.15.cloned.1.call-start = ((), (), s32[]{:S(2)}) async-start(), calls=%async_computation.12 | async-start | bytes 4644864 | tf_op jit(solution)/shard_map/reduce_scatter | solution.py:286
  805.1 7.3 collective-permute-start.4
  806.6 6.7 collective-permute-start.3
  807.9 6.1 collective-permute-start.2
  809.8 2.6 collective-permute-start.5
  904.8 223.3 %copy-start.25 = (f32[2,144,1728]{2,1,0:T(8,128)S(1)}, f32[2,144,1728]{2,1,0:T(8,128)}, u32[]{:S(2)}) copy-start(f32[2,144,1728]{2,1,0:T(8,128)} %param.34) | copy-start | bytes 5971972
  (93 other events, 2114.8 us)
Sparse Core Ops, SparseCore 0:
  12.4 57.0 all-gather.10
  229.9 57.9 all-reduce.12
  438.1 54.0 all-reduce.14
  514.1 55.7 all-reduce.16
  638.9 22.5 reduce-scatter.16
  665.5 62.1 reduce-scatter.12
  731.5 62.6 reduce-scatter.10
  796.7 57.8 all-reduce.18
  859.0 267.0 all-reduce.20
  1129.5 86.6 reduce-scatter.14
Sparse Core Ops, SparseCore 1:
  233.1 125.2 all-gather.6
  361.0 70.2 all-gather.8
where the time goes:
time: 1240 us; the launch traced here: 1230 us
  waiting for transfers between devices  697 us (56%)
  blocking collectives  274 us (22%)
  other arithmetic  78.2 us (6%)
  matrix products  70 us (6%)
  local copies, waits for them, and re-layouts  69.9 us (6%)
  starting transfers between devices  21.6 us (2%)
  between operations  18 us (1%)
    unnamed x18, waiting for transfers between devices  229 us
    psum x4, waiting for transfers between devices, reduce_model(): return lax.psum(local_sum, 'mp')  196 us
    unnamed x2, blocking collectives  127 us
    reduce_scatter x1, waiting for transfers between devices, on_device(): lax.psum_scatter(grad_down.astype(jnp.bfloat16), 'dp', scatter_dimension=...  81.3 us
    ppermute x6, waiting for transfers between devices, shifted(): return lax.ppermute(value, axis, pairs)  65.9 us
    all_gather x1, waiting for transfers between devices, on_device(): lax.all_gather(w_gateup.astype(bf), 'dp', axis=1, tiled=True)  64.1 us
    all_gather x1, waiting for transfers between devices, on_device(): lax.all_gather(w_down.astype(bf), 'dp', axis=1, tiled=True)  61 us
    all_gather x1, blocking collectives, on_device(): lax.all_gather(gain_heads.astype(bf), ('dp', 'mp'), axis=1, tiled=True)  43 us
  transfers between devices with their start and end apart: 22, of which 17 were waited for; matrix products, arithmetic and copies ran while one was open for 18% of the time, Pallas kernels for 0%

commit v1 on v0

v1 whole, which is shorter than its diff:
```python
import jax
import jax.numpy as jnp
from jax import lax
from jax.sharding import Mesh, PartitionSpec as P

HD = 256
SEQ = 2048
ADAM_STEP = 4


EPS = 1e-06
THETA = 1000000.0
LEARN = 0.02
BETA_ONE = 0.9
BETA_TWO = 0.95
ADAM_EPS = 1e-08
DECAY = 0.1
GELU_COEF = 0.7978845608028654
GELU_CUBE = 0.044715
NEG_FILL = -1e30

bf = jnp.bfloat16
fl = jnp.float32
DP = ("z", "y")


def rms_scale(values):
    return lax.rsqrt(jnp.mean(values * values, axis=-1, keepdims=True) + EPS)


def norm_back(values, scale, factor, incoming):
    scaled = incoming * factor
    return scale * (
        scaled - values * (scale * scale) * jnp.mean(scaled * values, axis=-1, keepdims=True)
    )


def rotate_half(values):
    middle = values.shape[-1] // 2
    return jnp.concatenate([-values[..., middle:], values[..., :middle]], axis=-1)


def rope_tables(position, width):
    middle = width // 2
    freqs = THETA ** (-2.0 * jnp.arange(middle, dtype=jnp.float32) / width)
    angle = position.astype(jnp.float32)[:, None] * freqs[None, :]
    cosine = jnp.concatenate([jnp.cos(angle), jnp.cos(angle)], axis=-1)
    sine = jnp.concatenate([jnp.sin(angle), jnp.sin(angle)], axis=-1)
    return (cosine, sine)


def gelu_parts(values):
    inner = GELU_COEF * (values + GELU_CUBE * values * values * values)
    tanh_val = jnp.tanh(inner)
    value = 0.5 * values * (1.0 + tanh_val)
    slope = 0.5 * (1.0 + tanh_val) + 0.5 * values * (1.0 - tanh_val * tanh_val) * GELU_COEF * (
        1.0 + 3.0 * GELU_CUBE * values * values
    )
    return (value, slope)


def adam_update(weight, mom, var, grad, decay):
    mom_new = BETA_ONE * mom + (1.0 - BETA_ONE) * grad
    var_new = BETA_TWO * var + (1.0 - BETA_TWO) * grad * grad
    fix_one = 1.0 - BETA_ONE**ADAM_STEP
    fix_two = 1.0 - BETA_TWO**ADAM_STEP
    direction = mom_new / fix_one / (jnp.sqrt(var_new / fix_two) + ADAM_EPS)
    return (weight - LEARN * (direction + decay * weight), mom_new, var_new)


def rotated(value, axis, by):
    size = lax.axis_size(axis)
    return lax.ppermute(value, axis, [(i, (i + by) % size) for i in range(size)])


def shifted(value, by):
    size = lax.axis_size(DP)
    return lax.ppermute(
        value, DP, [(i, i + by) for i in range(size) if 0 <= i + by < size]
    )


def pick(value, index):
    return lax.dynamic_index_in_dim(value, index, 0, keepdims=False)


def gather_axis(value, axis):
    size = lax.axis_size(axis)
    me = lax.axis_index(axis)
    if size == 2:
        other = rotated(value, axis, 1)
        return jnp.stack([jnp.where(me == 0, value, other), jnp.where(me == 0, other, value)])
    whole = jnp.zeros((size,) + value.shape, value.dtype)
    whole = lax.dynamic_update_index_in_dim(whole, value, me, 0)
    for by in range(1, size):
        whole = lax.dynamic_update_index_in_dim(
            whole, rotated(value, axis, by), (me - by) % size, 0
        )
    return whole


def scatter_axis(pieces, axis):
    size = lax.axis_size(axis)
    me = lax.axis_index(axis)
    total = pick(pieces, me).astype(fl)
    for by in range(1, size):
        sent = pick(pieces, (me + by) % size).astype(bf)
        total = total + rotated(sent, axis, by).astype(fl)
    return total


def scatter_model(partial):
    xs, cs = lax.axis_size("x"), lax.axis_size("c")
    rows, width = partial.shape
    view = partial.reshape(xs, cs, rows // (xs * cs), width)
    half = scatter_axis(view.swapaxes(0, 1), "c")
    return scatter_axis(half, "x")


def gather_model(part):
    both = gather_axis(part, "x")
    four = gather_axis(both, "c")
    four = four.swapaxes(0, 1)
    return four.reshape((-1,) + part.shape[1:])


def ring_order(size):
    return [0, 1, 3, 2] if size == 4 else list(range(size))


def ring_step(value):
    order = ring_order(lax.axis_size("z"))
    size = len(order)
    return lax.ppermute(value, "z", [(order[i], order[(i + 1) % size]) for i in range(size)])


def ring_place():
    order = ring_order(lax.axis_size("z"))
    place = [order.index(i) for i in range(len(order))]
    return jnp.array(order), pick(jnp.array(place), lax.axis_index("z"))


def gather_weights(block):
    order, place = ring_place()
    zs, ys = lax.axis_size("z"), lax.axis_size("y")
    kinds, rows, width = block.shape
    whole = jnp.zeros((kinds, zs * ys * rows, width), block.dtype)
    me = lax.axis_index("y")
    moving = block
    for step in range(zs):
        source = pick(order, (place - step) % zs)
        for by in range(ys):
            piece = moving if by == 0 else rotated(moving, "y", by)
            start = (source * ys + (me - by) % ys) * rows
            whole = lax.dynamic_update_slice_in_dim(whole, piece, start, 1)
        if step < zs - 1:
            moving = ring_step(moving)
    return whole


def scatter_weights(grads):
    order, place = ring_place()
    zs, ys = lax.axis_size("z"), lax.axis_size("y")
    kinds, total, width = grads.shape
    rows = total // (zs * ys)
    me = lax.axis_index("y")

    def summed(target):
        def piece(by):
            start = (target * ys + (me + by) % ys) * rows
            return lax.dynamic_slice_in_dim(grads, start, rows, 1).astype(bf)

        result = piece(0).astype(fl)
        for by in range(1, ys):
            result = result + rotated(piece(by), "y", by).astype(fl)
        return result

    running = summed(pick(order, (place - 1) % zs))
    for step in range(zs - 1):
        moved = ring_step(running.astype(bf))
        running = moved.astype(fl) + summed(pick(order, (place - step - 2) % zs))
    return running


def on_device(
    block_in,
    out_grad,
    segment_ids,
    w_query,
    w_keyval,
    w_out,
    w_gateup,
    w_down,
    gain_layers,
    gain_heads,
    mom_query,
    var_query,
    mom_keyval,
    var_keyval,
    mom_out,
    var_out,
    mom_gateup,
    var_gateup,
    mom_down,
    var_down,
    mom_layers,
    var_layers,
    mom_heads,
    var_heads,
):
    zs, ys = lax.axis_size("z"), lax.axis_size("y")
    xs, cs = lax.axis_size("x"), lax.axis_size("c")
    dps, mps = zs * ys, xs * cs
    model = lax.axis_index("x") * cs + lax.axis_index("c")
    device = lax.axis_index("z") * ys + lax.axis_index("y")
    width = HD
    rows, depth = block_in.shape
    quarter = rows // mps
    factor = width ** (-0.5)
    norm_factor = float(rows * dps) ** (-0.5)
    drows = w_query.shape[0]
    krows = w_keyval.shape[0]
    gcols, hcols = gain_layers.shape[1], gain_heads.shape[1]

    small = jnp.concatenate([gain_layers.reshape(-1), gain_heads.reshape(-1)]).astype(bf)
    small = jnp.pad(small, (0, width - small.shape[0])).reshape(1, width)
    keyval_halves = jnp.concatenate([w_keyval[:, :width], w_keyval[:, width:]], axis=0).astype(bf)
    pack = jnp.concatenate(
        [w_query.astype(bf), w_out.T.astype(bf), keyval_halves, small], axis=0
    )
    by_z = gather_axis(pack, "z")
    by_dp = gather_axis(by_z, "y").swapaxes(0, 1).reshape((dps,) + pack.shape)
    low_query = by_dp[:, :drows].reshape(depth, width)
    low_out = by_dp[:, drows : 2 * drows].reshape(depth, width)
    kv_mine = by_dp[:, 2 * drows :]
    kv_all = gather_axis(gather_axis(kv_mine, "x"), "c").swapaxes(0, 1)
    kv_all = kv_all.reshape((mps,) + kv_mine.shape).swapaxes(0, 1)
    low_key = kv_all[:, :, :krows].reshape(depth, width)
    low_value = kv_all[:, :, krows : 2 * krows].reshape(depth, width)
    gains = kv_all[:, :, 2 * krows].astype(fl)
    gain_scale = 1.0 + gains[:, :, : 4 * gcols].reshape(dps, mps, 4, gcols).transpose(
        2, 0, 1, 3
    ).reshape(4, depth)
    head_scale = 1.0 + gains[:, :, 4 * gcols : 4 * gcols + 2 * hcols].reshape(
        dps, mps, 2, hcols
    ).transpose(2, 0, 1, 3).reshape(2, width)
    low_keyval = jnp.concatenate([low_key, low_value], axis=1)

    low_ffn = gather_weights(
        jnp.concatenate([w_gateup.astype(bf), w_down.T.astype(bf)[None]], axis=0)
    )

    margin = SEQ // 2
    first_row = device * rows
    shifted_first = first_row + margin
    seq_start = shifted_first // SEQ * SEQ
    span = SEQ // rows
    position = shifted_first + jnp.arange(rows, dtype=jnp.int32)
    cosine, sine = rope_tables(position % SEQ, width)

    def part_rows(values):
        return lax.dynamic_slice_in_dim(values, model * quarter, quarter, 0)

    scale_in = rms_scale(block_in)
    normed_in = (block_in * scale_in * gain_scale[0]).astype(bf)
    keyval_raw = jnp.dot(normed_in, low_keyval, preferred_element_type=fl)
    key_raw = keyval_raw[:, :width]
    scale_key = rms_scale(key_raw)
    key_norm = key_raw * scale_key * head_scale[1]
    key_rot = key_norm * cosine + rotate_half(key_norm) * sine
    keyval_low = jnp.concatenate([key_rot, keyval_raw[:, width:]], axis=1).astype(bf)
    sent_kv = part_rows(keyval_low)
    earlier = jnp.stack([shifted(sent_kv, by) for by in range(span - 1, 0, -1)])
    four = gather_axis(gather_axis(earlier, "x"), "c")
    earlier = four.transpose(2, 1, 0, 3, 4).reshape((span - 1) * rows, 2 * width)
    window = jnp.concatenate([earlier, keyval_low], axis=0)
    seq_keys, seq_values = window[:, :width], window[:, width:]

    query_raw = jnp.dot(normed_in, low_query, preferred_element_type=fl)
    scale_query = rms_scale(query_raw)
    query_norm = query_raw * scale_query * head_scale[0]
    query_rot = (query_norm * cosine + rotate_half(query_norm) * sine).astype(bf)

    padded_seg = jnp.pad(segment_ids, (SEQ, 0), constant_values=-1)
    seg_query = lax.dynamic_slice_in_dim(segment_ids, first_row, rows, 0)
    reach = span * rows
    seg_keys = lax.dynamic_slice_in_dim(padded_seg, first_row + rows + SEQ - reach, reach, 0)
    key_index = shifted_first + rows - reach + jnp.arange(reach, dtype=jnp.int32)
    allowed = (
        (key_index[None, :] <= position[:, None])
        & (key_index[None, :] >= seq_start)
        & (seg_keys[None, :] == seg_query[:, None])
    )
    scores = jnp.einsum("qd,kd->qk", query_rot, seq_keys, preferred_element_type=fl) * factor
    masked = jnp.where(allowed, scores, NEG_FILL)
    top = jnp.max(masked, axis=-1, keepdims=True)
    log_total = top + jnp.log(jnp.sum(jnp.exp(masked - top), axis=-1, keepdims=True))
    probs = jnp.exp(masked - log_total)
    probs_low = probs.astype(bf)
    attended = jnp.dot(probs_low, seq_values, preferred_element_type=fl).astype(bf)

    in_part, scale_in_part = part_rows(block_in), part_rows(scale_in)
    grad_part = part_rows(out_grad)
    attn_proj = scatter_model(
        jnp.einsum("tc,dc->td", attended, low_out, preferred_element_type=fl)
    )
    scale_attn = rms_scale(attn_proj)
    resid = in_part + attn_proj * scale_attn * gain_scale[1]
    scale_mid = rms_scale(resid)
    normed_mid = gather_model((resid * scale_mid * gain_scale[2]).astype(bf))
    gate_raw = jnp.dot(normed_mid, low_ffn[0], preferred_element_type=fl)
    up_raw = jnp.dot(normed_mid, low_ffn[1], preferred_element_type=fl)
    gelu_value, gelu_slope = gelu_parts(gate_raw)
    hidden = (gelu_value * up_raw).astype(bf)
    ffn_proj = scatter_model(
        jnp.einsum("tf,df->td", hidden, low_ffn[2], preferred_element_type=fl)
    )
    scale_ffn = rms_scale(ffn_proj)
    out_part = resid + ffn_proj * scale_ffn * gain_scale[3]
    grad_ffn = gather_model(norm_back(ffn_proj, scale_ffn, gain_scale[3], grad_part).astype(bf))
    block_out = gather_model(out_part.astype(bf)).astype(fl)
    grad_down = jnp.einsum("td,tf->df", grad_ffn, hidden, preferred_element_type=fl).astype(bf)
    sum_down = scatter_weights(grad_down[None])[0].T
    grad_hidden = jnp.dot(grad_ffn, low_ffn[2], preferred_element_type=fl)
    grad_gate = (grad_hidden * up_raw * gelu_slope).astype(bf)
    grad_up = (grad_hidden * gelu_value).astype(bf)
    grad_mid = scatter_model(
        jnp.einsum("tf,df->td", grad_gate, low_ffn[0], preferred_element_type=fl)
        + jnp.einsum("tf,df->td", grad_up, low_ffn[1], preferred_element_type=fl)
    )
    grad_gateup = jnp.stack(
        [
            jnp.einsum("td,tf->df", normed_mid, grad_gate, preferred_element_type=fl).astype(bf),
            jnp.einsum("td,tf->df", normed_mid, grad_up, preferred_element_type=fl).astype(bf),
        ]
    )
    sum_gateup = scatter_weights(grad_gateup)
    grad_resid = grad_part + norm_back(resid, scale_mid, gain_scale[2], grad_mid)
    grad_attn = gather_model(
        norm_back(attn_proj, scale_attn, gain_scale[1], grad_resid).astype(bf)
    )
    grad_out = jnp.einsum("td,tc->dc", grad_attn, attended, preferred_element_type=fl)
    grad_attended = jnp.dot(grad_attn, low_out, preferred_element_type=fl).astype(bf)
    row_delta = jnp.sum(grad_attended.astype(fl) * attended.astype(fl), axis=-1, keepdims=True)
    grad_probs = jnp.einsum("qd,kd->qk", grad_attended, seq_values, preferred_element_type=fl)
    grad_scores = (probs * (grad_probs - row_delta) * factor).astype(bf)
    grad_qrot = jnp.dot(grad_scores, seq_keys, preferred_element_type=fl)
    grad_krot_seq = jnp.einsum("qk,qd->kd", grad_scores, query_rot, preferred_element_type=fl)
    grad_values_seq = jnp.einsum("qk,qd->kd", probs_low, grad_attended, preferred_element_type=fl)
    grad_seq = jnp.concatenate([grad_krot_seq, grad_values_seq], axis=1)
    by_model = grad_seq.reshape(span, xs, cs, quarter, 2 * width).transpose(2, 1, 0, 3, 4)
    by_block = scatter_axis(scatter_axis(by_model, "c"), "x")
    grad_kpart = by_block[span - 1]
    for by in range(1, span):
        grad_kpart = grad_kpart + shifted(by_block[span - 1 - by].astype(bf), -by).astype(fl)

    cos_part, sin_part = part_rows(cosine), part_rows(sine)
    key_part, scale_kpart = part_rows(key_raw), part_rows(scale_key)
    grad_krot = grad_kpart[:, :width]
    key_back = grad_krot * cos_part - rotate_half(grad_krot * sin_part)
    grad_kin = norm_back(key_part, scale_kpart, head_scale[1], key_back)
    grad_kvin = jnp.concatenate([grad_kin, grad_kpart[:, width:]], axis=1).astype(bf)
    keyval_part = jnp.einsum("tc,dc->td", grad_kvin, low_keyval, preferred_element_type=fl)
    grad_keyval = jnp.einsum(
        "td,tc->dc", normed_in, gather_model(grad_kvin), preferred_element_type=fl
    )
    grad_keyval = pick(grad_keyval.reshape(dps, mps, krows, 2 * width).swapaxes(0, 1), model)

    query_back = grad_qrot * cosine - rotate_half(grad_qrot * sine)
    grad_qin = norm_back(query_raw, scale_query, head_scale[0], query_back).astype(bf)
    grad_query = jnp.einsum("td,tc->dc", normed_in, grad_qin, preferred_element_type=fl)
    grad_normed = scatter_model(
        jnp.einsum("tc,dc->td", grad_qin, low_query, preferred_element_type=fl)
    ) + keyval_part
    grad_in_part = grad_resid + norm_back(in_part, scale_in_part, gain_scale[0], grad_normed)
    grad_input = gather_model(grad_in_part.astype(bf)).astype(fl)

    grad_layers = jnp.stack(
        [
            jnp.sum(grad_normed * in_part * scale_in_part, axis=0),
            jnp.sum(grad_resid * attn_proj * scale_attn, axis=0),
            jnp.sum(grad_mid * resid * scale_mid, axis=0),
            jnp.sum(grad_part * ffn_proj * scale_ffn, axis=0),
        ]
    )
    grad_heads = jnp.stack(
        [
            jnp.sum(query_back * query_raw * scale_query, axis=0),
            jnp.sum(key_back * key_part * scale_kpart, axis=0),
        ]
    )
    grad_small = jnp.concatenate(
        [
            grad_layers.reshape(4, dps, mps, gcols).transpose(1, 2, 0, 3).reshape(dps, mps, -1),
            grad_heads.reshape(2, dps, mps, hcols).transpose(1, 2, 0, 3).reshape(dps, mps, -1),
        ],
        axis=2,
    )
    grad_small = jnp.pad(grad_small, ((0, 0), (0, 0), (0, width - grad_small.shape[2])))
    grad_small = grad_small.reshape(dps, xs, cs, width).transpose(2, 1, 0, 3)
    grad_small = scatter_axis(scatter_axis(grad_small, "c"), "x")
    grad_pack = jnp.concatenate(
        [
            grad_query.reshape(dps, drows, width).astype(bf),
            grad_out.reshape(dps, drows, width).astype(bf),
            grad_keyval[:, :, :width].astype(bf),
            grad_keyval[:, :, width:].astype(bf),
            grad_small[:, None].astype(bf),
        ],
        axis=1,
    )
    sums_pack = scatter_axis(
        scatter_axis(grad_pack.reshape((zs, ys) + grad_pack.shape[1:]).swapaxes(0, 1), "y"), "z"
    )
    sum_query = sums_pack[:drows]
    sum_out = sums_pack[drows : 2 * drows].T
    sum_keyval = jnp.concatenate(
        [
            sums_pack[2 * drows : 2 * drows + krows],
            sums_pack[2 * drows + krows : 2 * drows + 2 * krows],
        ],
        axis=1,
    )
    sum_small = sums_pack[2 * drows + 2 * krows]
    sum_layers = sum_small[: 4 * gcols].reshape(4, gcols)
    sum_heads = sum_small[4 * gcols : 4 * gcols + 2 * hcols].reshape(2, hcols)

    masters = (w_query, w_keyval, w_out, w_gateup, w_down, gain_layers, gain_heads)
    sums = (sum_query, sum_keyval, sum_out, sum_gateup, sum_down, sum_layers, sum_heads)
    totals = tuple((item * norm_factor for item in sums))
    moms = (mom_query, mom_keyval, mom_out, mom_gateup, mom_down, mom_layers, mom_heads)
    varis = (var_query, var_keyval, var_out, var_gateup, var_down, var_layers, var_heads)
    decays = (DECAY, DECAY, DECAY, DECAY, DECAY, 0.0, 0.0)
    updated = [
        adam_update(master, mom, var, grad, decay)
        for master, mom, var, grad, decay in zip(masters, moms, varis, totals, decays)
    ]
    return (
        (block_out, grad_input)
        + totals
        + tuple(item[0] for item in updated)
        + tuple(item[1] for item in updated)
        + tuple(item[2] for item in updated)
    )


def solution(mesh):
    dps, mps = mesh.shape["dp"], mesh.shape["mp"]
    zs = 4 if dps % 4 == 0 else 1
    cs = 2 if mps % 2 == 0 else 1
    split = Mesh(mesh.devices.reshape(zs, dps // zs, mps // cs, cs), ("z", "y", "x", "c"))
    mp = ("x", "c")
    both = DP + mp
    weights = (
        P(DP, mp),
        P(both, None),
        P(mp, DP),
        P(None, DP, mp),
        P(mp, DP),
        P(None, both),
        P(None, both),
    )
    tokens = P(DP, None)
    states = tuple(spec for spec in weights for _ in range(2))
    in_specs = (tokens, tokens, P()) + weights + states
    out_specs = (tokens, tokens) + weights * 4
    return jax.shard_map(
        on_device, mesh=split, in_specs=in_specs, out_specs=out_specs, check_vma=False
    )
```

time: 1240 us -> 899 us (0.72)
  waiting for transfers between devices: 697 us -> 304 us
  local copies, waits for them, and re-layouts: 69.9 us -> 355 us
  blocking collectives: 274 us -> 0 us
  starting transfers between devices: 21.6 us -> 71.9 us
  matrix products: 70 us -> 54 us
    ppermute x6 -> x63, waiting for transfers between devices: 65.9 us -> 304 us  [the longest x48 193 us: rotated(): lax.ppermute(value, axis, [(i, (i + by) % size) for i in range(size)])]
    dynamic_update_slice x1 -> x13, local copies, waits for them, and re-layouts: 0.04 us -> 235 us  [the longest x8 231 us: gather_weights(): whole = lax.dynamic_update_slice_in_dim(whole, piece, start, 1)]
    unnamed x18 -> x0, waiting for transfers between devices: 229 us -> none
    psum x4 -> x0, waiting for transfers between devices: 196 us -> none  [reduce_model(): return lax.psum(local_sum, 'mp')]
    all_gather x4 -> x0, blocking collectives: 147 us -> none  [the longest x1 43 us: on_device(): lax.all_gather(gain_heads.astype(bf), ('dp', 'mp'), axis=1, tiled=True)]
    unnamed x2 -> x0, blocking collectives: 127 us -> none
    all_gather x3 -> x0, waiting for transfers between devices: 125 us -> none  [the longest x1 64.1 us: on_device(): lax.all_gather(w_gateup.astype(bf), 'dp', axis=1, tiled=True)]
    reduce_scatter x3 -> x0, waiting for transfers between devices: 81.3 us -> none  [the longest x1 81.3 us: on_device(): lax.psum_scatter(grad_down.astype(jnp.bfloat16), 'dp', scatter_dimension=...]
  transfers between devices with their start and end apart: 22 -> 63, of which waited for: 17 -> 29; matrix products, arithmetic and copies ran while one was open for 18% -> 42% of each run, Pallas kernels for 0% -> 0%
where the time goes in v1:
time: 899 us; the launch traced here: 883 us
  local copies, waits for them, and re-layouts  355 us (39%)
  waiting for transfers between devices  304 us (34%)
  other arithmetic  82.4 us (9%)
  starting transfers between devices  71.9 us (8%)
  matrix products  54 us (6%)
  between operations  15.1 us (2%)
    dynamic_update_slice x8, local copies, waits for them, and re-layouts, gather_weights(): whole = lax.dynamic_update_slice_in_dim(whole, piece, start, 1)  231 us
    ppermute x48, waiting for transfers between devices, rotated(): lax.ppermute(value, axis, [(i, (i + by) % size) for i in range(size)])  193 us
    ppermute x9, waiting for transfers between devices, ring_step(): lax.ppermute(value, 'z', [(order[i], order[(i + 1) % size]) for i in rang...  105 us
    ppermute x48, starting transfers between devices, rotated(): lax.ppermute(value, axis, [(i, (i + by) % size) for i in range(size)])  41.8 us
    unnamed x229, local copies, waits for them, and re-layouts  18.4 us
  transfers between devices with their start and end apart: 63, of which 29 were waited for; matrix products, arithmetic and copies ran while one was open for 42% of the time, Pallas kernels for 0%

profile of v1, /device:TPU:0, one launch (start us, length us, event | category | flops | bytes accessed | tf_op | source)
XLA Modules:
  0.0 882.7 jit_solution(6962742459649798351)
XLA Ops:
  27.3 16.9 %collective-permute-done.3 = bf16[4,361,256]{2,0,1:T(4,128)(2,1)} collective-permute-done((bf16[4,361,256]{2,0,1:T(4,128)(2,1)}, bf16[4,361,256]{2,0,1:T(4,128)(2,1)}, u32[]{:S(2)}, u32[]{:S(2)}) %collective-permute-start.3) | collective-permute-done | bytes 739360 | tf_op jit(solution)/shard_map/ppermute | solution.py:73
  47.4 7.2 collective-permute-done.4
  92.8 8.8 collective-permute-done.9
  115.6 27.4 %collective-permute-done.16 = bf16[3,144,1728]{2,1,0:T(8,128)(2,1)} collective-permute-done((bf16[3,144,1728]{2,1,0:T(8,128)(2,1)}, bf16[3,144,1728]{2,1,0:T(8,128)(2,1)}, u32[]{:S(2)}, u32[]{:S(2)}) %collective-permute-start.16) | collective-permute-done | bytes 1493024 | tf_op jit(solution)/shard_map/ppermute | solution.py:134
  151.9 28.8 %collective-permute-done.18 = bf16[3,144,1728]{2,1,0:T(8,128)(2,1)} collective-permute-done((bf16[3,144,1728]{2,1,0:T(8,128)(2,1)}, bf16[3,144,1728]{2,1,0:T(8,128)(2,1)}, u32[]{:S(2)}, u32[]{:S(2)}) %collective-permute-start.18) | collective-permute-done | bytes 1493024 | tf_op jit(solution)/shard_map/ppermute | solution.py:134
  193.6 23.6 %collective-permute-done.20 = bf16[3,144,1728]{2,1,0:T(8,128)(2,1)} collective-permute-done((bf16[3,144,1728]{2,1,0:T(8,128)(2,1)}, bf16[3,144,1728]{2,1,0:T(8,128)(2,1)}, u32[]{:S(2)}, u32[]{:S(2)}) %collective-permute-start.20) | collective-permute-done | bytes 1493024 | tf_op jit(solution)/shard_map/ppermute | solution.py:134
  239.5 25.9 %dynamic_update_slice.41 = bf16[3,1152,1728]{1,2,0:T(8,128)(2,1)} dynamic-update-slice(bf16[3,1152,1728]{1,2,0:T(8,128)(2,1)} %broadcast_in_dim.29, bf16[3,144,1728]{1,2,0:T(8,128)(2,1)} %copy.554, s32[]{:T(128)} %constant.512.clone.1, s32[]{:T(128)S(6)} %select_n.593, s32[]{:T(128)} %constant.512.clone.1) | dynamic-update-slice | bytes 2985988 | tf_op jit(solution)/shard_map/dynamic_update_slice | solution.py:155
  269.4 29.5 %dynamic_update_slice.42 = bf16[3,1152,1728]{1,2,0:T(8,128)(2,1)} dynamic-update-slice(bf16[3,1152,1728]{1,2,0:T(8,128)(2,1)} %dynamic_update_slice.41, bf16[3,144,1728]{1,2,0:T(8,128)(2,1)} %copy.555, s32[]{:T(128)} %constant.512.clone.1, s32[]{:T(128)S(6)} %select_n.595, s32[]{:T(128)} %constant.512.clone.1) | dynamic-update-slice | bytes 2985988 | tf_op jit(solution)/shard_map/dynamic_update_slice | solution.py:155
  302.9 29.5 %dynamic_update_slice.43 = bf16[3,1152,1728]{1,2,0:T(8,128)(2,1)} dynamic-update-slice(bf16[3,1152,1728]{1,2,0:T(8,128)(2,1)} %dynamic_update_slice.42, bf16[3,144,1728]{1,2,0:T(8,128)(2,1)} %copy.556, s32[]{:T(128)} %constant.512.clone.1, s32[]{:T(128)S(6)} %select_n.598, s32[]{:T(128)} %constant.512.clone.1) | dynamic-update-slice | bytes 2985988 | tf_op jit(solution)/shard_map/dynamic_update_slice | solution.py:155
  336.3 29.5 %dynamic_update_slice.44 = bf16[3,1152,1728]{1,2,0:T(8,128)(2,1)} dynamic-update-slice(bf16[3,1152,1728]{1,2,0:T(8,128)(2,1)} %dynamic_update_slice.43, bf16[3,144,1728]{1,2,0:T(8,128)(2,1)} %copy.557, s32[]{:T(128)} %constant.512.clone.1, s32[]{:T(128)S(6)} %select_n.599, s32[]{:T(128)} %constant.512.clone.1) | dynamic-update-slice | bytes 2985988 | tf_op jit(solution)/shard_map/dynamic_update_slice | solution.py:155
  369.8 29.3 %dynamic_update_slice.45 = bf16[3,1152,1728]{1,2,0:T(8,128)(2,1)} dynamic-update-slice(bf16[3,1152,1728]{1,2,0:T(8,128)(2,1)} %dynamic_update_slice.44, bf16[3,144,1728]{1,2,0:T(8,128)(2,1)} %copy.558, s32[]{:T(128)} %constant.512.clone.1, s32[]{:T(128)S(6)} %select_n.602, s32[]{:T(128)} %constant.512.clone.1) | dynamic-update-slice | bytes 2985988 | tf_op jit(solution)/shard_map/dynamic_update_slice | solution.py:155
  403.1 28.7 %dynamic_update_slice.46 = bf16[3,1152,1728]{1,2,0:T(8,128)(2,1)} dynamic-update-slice(bf16[3,1152,1728]{1,2,0:T(8,128)(2,1)} %dynamic_update_slice.45, bf16[3,144,1728]{1,2,0:T(8,128)(2,1)} %copy.559, s32[]{:T(128)} %constant.512.clone.1, s32[]{:T(128)S(6)} %select_n.603, s32[]{:T(128)} %constant.512.clone.1) | dynamic-update-slice | bytes 2985988 | tf_op jit(solution)/shard_map/dynamic_update_slice | solution.py:155
  435.8 29.5 %dynamic_update_slice.47 = bf16[3,1152,1728]{1,2,0:T(8,128)(2,1)} dynamic-update-slice(bf16[3,1152,1728]{1,2,0:T(8,128)(2,1)} %dynamic_update_slice.46, bf16[3,144,1728]{1,2,0:T(8,128)(2,1)} %copy.560, s32[]{:T(128)} %constant.512.clone.1, s32[]{:T(128)S(6)} %select_n.606, s32[]{:T(128)} %constant.512.clone.1) | dynamic-update-slice | bytes 2985988 | tf_op jit(solution)/shard_map/dynamic_update_slice | solution.py:155
  471.9 29.5 %dynamic_update_slice.48 = bf16[3,1152,1728]{1,2,0:T(8,128)(2,1)} dynamic-update-slice(bf16[3,1152,1728]{1,2,0:T(8,128)(2,1)} %dynamic_update_slice.47, bf16[3,144,1728]{1,2,0:T(8,128)(2,1)} %copy.561, s32[]{:T(128)} %constant.512.clone.1, s32[]{:T(128)S(6)} %select_n.607, s32[]{:T(128)} %constant.512.clone.1) | dynamic-update-slice | bytes 2985988 | tf_op jit(solution)/shard_map/dynamic_update_slice | solution.py:155
  506.6 9.1 %multiply_convert_fusion.2 = (bf16[512,1728]{0,1:T(8,128)(2,1)}, f32[512,1728]{0,1:T(8,128)}) fusion(f32[512,1728]{0,1:T(8,128)S(1)} %fusion.15, bf16[512,1152]{1,0:T(8,128)(2,1)S(1)} %bitcast.452, bf16[3,1152,1728]{1,2,0:T(8,128)(2,1)} %dynamic_update_slice.48), kind=kOutput, calls=%fused_computation.43 | convolution fusion | flops 2047279104 | bytes 14008320 | tf_op jit(solution)/shard_map/dot_general | solution.py:312
  599.1 81.4 %collective-permute-done.56 = bf16[1,144,1728]{2,1,0:T(8,128)(2,1)S(1)} collective-permute-done((bf16[1,144,1728]{2,1,0:T(8,128)(2,1)S(1)}, bf16[1,144,1728]{2,1,0:T(8,128)(2,1)S(1)}, u32[]{:S(2)}, u32[]{:S(2)}) %collective-permute-start.56) | collective-permute-done | bytes 497696 | tf_op jit(solution)/shard_map/ppermute | solution.py:73
  681.9 7.0 collective-permute-done.29
  773.0 7.3 collective-permute-done.35
  783.1 9.4 %collective-permute-done.52 = bf16[2,144,1728]{2,1,0:T(8,128)(2,1)S(1)} collective-permute-done((bf16[2,144,1728]{2,1,0:T(8,128)(2,1)S(1)}, bf16[2,144,1728]{2,1,0:T(8,128)(2,1)S(1)}, u32[]{:S(2)}, u32[]{:S(2)}) %collective-permute-start.52) | collective-permute-done | bytes 995360 | tf_op jit(solution)/shard_map/ppermute | solution.py:134
  816.1 9.1 %collective-permute-done.41 = bf16[128,512]{1,0:T(8,128)(2,1)S(1)} collective-permute-done((bf16[128,512]{1,0:T(8,128)(2,1)S(1)}, bf16[128,512]{1,0:T(8,128)(2,1)S(1)}, u32[]{:S(2)}, u32[]{:S(2)}) %collective-permute-start.41) | collective-permute-done | bytes 131104 | tf_op jit(solution)/shard_map/ppermute | solution.py:73
  830.1 6.9 concatenate.87
  838.8 7.8 multiply_subtract_fusion
  846.7 11.0 %collective-permute-done.45 = bf16[4,361,256]{2,0,1:T(4,128)(2,1)S(1)} collective-permute-done((bf16[4,361,256]{2,0,1:T(4,128)(2,1)S(1)}, bf16[4,361,256]{2,0,1:T(4,128)(2,1)S(1)}, u32[]{:S(2)}, u32[]{:S(2)}) %collective-permute-start.45) | collective-permute-done | bytes 739360 | tf_op jit(solution)/shard_map/ppermute | solution.py:73
  864.5 13.3 %collective-permute-done.47 = bf16[361,256]{1,0:T(8,128)(2,1)S(1)} collective-permute-done((bf16[361,256]{1,0:T(8,128)(2,1)S(1)}, bf16[361,256]{1,0:T(8,128)(2,1)S(1)}, u32[]{:S(2)}, u32[]{:S(2)}) %collective-permute-start.47) | collective-permute-done | bytes 184864 | tf_op jit(solution)/shard_map/ppermute | solution.py:73
  (594 shorter events, 361.4 us)
Async XLA Ops:
  25.6 18.7 %collective-permute-start.3 = (bf16[4,361,256]{2,0,1:T(4,128)(2,1)}, bf16[4,361,256]{2,0,1:T(4,128)(2,1)}, u32[]{:S(2)}, u32[]{:S(2)}) collective-permute-start(bf16[4,361,256]{2,0,1:T(4,128)(2,1)} %copy.538), channel_id=1, source_target_pairs={{0,4},{4,0},{1,5},{5,1},{2,6},{6,2},{3,7},{7,3},{8,12},{12,8},{9,1... | collective-permute-start | bytes 2217992 | tf_op jit(solution)/shard_map/ppermute | solution.py:73
  104.0 39.0 %collective-permute-start.16 = (bf16[3,144,1728]{2,1,0:T(8,128)(2,1)}, bf16[3,144,1728]{2,1,0:T(8,128)(2,1)}, u32[]{:S(2)}, u32[]{:S(2)}) collective-permute-start(bf16[3,144,1728]{2,1,0:T(8,128)(2,1)} %pad_maximum_fusion.1), channel_id=1, source_target_pairs={{0,8},{8,24},{24,16},{16,0},{1,9},{9,25},{25,17},{17,1},{2,10},{10... | collective-permute-start | bytes 4478984 | tf_op jit(solution)/shard_map/ppermute | solution.py:134
  115.4 30.3 %collective-permute-start.11 = (bf16[2,128,1152]{2,1,0:T(8,128)(2,1)S(1)}, bf16[2,128,1152]{2,1,0:T(8,128)(2,1)S(1)}, u32[]{:S(2)}, u32[]{:S(2)}) collective-permute-start(bf16[2,128,1152]{2,1,0:T(8,128)(2,1)S(1)} %fusion.50), channel_id=1, source_target_pairs={{0,1},{1,0},{2,3},{3,2},{4,5},{5,4},{6,7},{7,6},{8,9},{9,8},{10,11... | collective-permute-start | bytes 1769480 | tf_op jit(solution)/shard_map/ppermute | solution.py:73
  143.0 37.7 %collective-permute-start.18 = (bf16[3,144,1728]{2,1,0:T(8,128)(2,1)}, bf16[3,144,1728]{2,1,0:T(8,128)(2,1)}, u32[]{:S(2)}, u32[]{:S(2)}) collective-permute-start(bf16[3,144,1728]{2,1,0:T(8,128)(2,1)} %collective-permute-done.16), channel_id=1, source_target_pairs={{0,8},{8,24},{24,16},{16,0},{1,9},{9,25},{25,17},{17,1},{2,10},{10... | collective-permute-start | bytes 4478984 | tf_op jit(solution)/shard_map/ppermute | solution.py:134
  148.1 34.3 %collective-permute-start.12 = (bf16[128,1152]{1,0:T(8,128)(2,1)S(1)}, bf16[128,1152]{1,0:T(8,128)(2,1)S(1)}, u32[]{:S(2)}, u32[]{:S(2)}) collective-permute-start(bf16[128,1152]{1,0:T(8,128)(2,1)S(1)} %fusion.64), channel_id=1, source_target_pairs={{0,2},{2,0},{1,3},{3,1},{4,6},{6,4},{5,7},{7,5},{8,10},{10,8},{9,1... | collective-permute-start | bytes 884744 | tf_op jit(solution)/shard_map/ppermute | solution.py:73
  180.7 36.4 %collective-permute-start.20 = (bf16[3,144,1728]{2,1,0:T(8,128)(2,1)}, bf16[3,144,1728]{2,1,0:T(8,128)(2,1)}, u32[]{:S(2)}, u32[]{:S(2)}) collective-permute-start(bf16[3,144,1728]{2,1,0:T(8,128)(2,1)} %collective-permute-done.18), channel_id=1, source_target_pairs={{0,8},{8,24},{24,16},{16,0},{1,9},{9,25},{25,17},{17,1},{2,10},{10... | collective-permute-start | bytes 4478984 | tf_op jit(solution)/shard_map/ppermute | solution.py:134
  187.3 78.1 %collective-permute-start.15 = (bf16[3,144,1728]{2,1,0:T(8,128)(2,1)}, bf16[3,144,1728]{2,1,0:T(8,128)(2,1)}, u32[]{:S(2)}, u32[]{:S(2)}) collective-permute-start(bf16[3,144,1728]{2,1,0:T(8,128)(2,1)} %pad_maximum_fusion.1), channel_id=1, source_target_pairs={{0,4},{4,0},{1,5},{5,1},{2,6},{6,2},{3,7},{7,3},{8,12},{12,8},{9,1... | collective-permute-start | bytes 4478984 | tf_op jit(solution)/shard_map/ppermute | solution.py:73
  187.3 145.0 %collective-permute-start.17 = (bf16[3,144,1728]{2,1,0:T(8,128)(2,1)}, bf16[3,144,1728]{2,1,0:T(8,128)(2,1)}, u32[]{:S(2)}, u32[]{:S(2)}) collective-permute-start(bf16[3,144,1728]{2,1,0:T(8,128)(2,1)} %collective-permute-done.16), channel_id=1, source_target_pairs={{0,4},{4,0},{1,5},{5,1},{2,6},{6,2},{3,7},{7,3},{8,12},{12,8},{9,1... | collective-permute-start | bytes 4478984 | tf_op jit(solution)/shard_map/ppermute | solution.py:73
  189.4 209.7 %collective-permute-start.19 = (bf16[3,144,1728]{2,1,0:T(8,128)(2,1)}, bf16[3,144,1728]{2,1,0:T(8,128)(2,1)}, u32[]{:S(2)}, u32[]{:S(2)}) collective-permute-start(bf16[3,144,1728]{2,1,0:T(8,128)(2,1)} %collective-permute-done.18), channel_id=1, source_target_pairs={{0,4},{4,0},{1,5},{5,1},{2,6},{6,2},{3,7},{7,3},{8,12},{12,8},{9,1... | collective-permute-start | bytes 4478984 | tf_op jit(solution)/shard_map/ppermute | solution.py:73
  217.1 250.8 %collective-permute-start.21 = (bf16[3,144,1728]{2,1,0:T(8,128)(2,1)}, bf16[3,144,1728]{2,1,0:T(8,128)(2,1)}, u32[]{:S(2)}, u32[]{:S(2)}) collective-permute-start(bf16[3,144,1728]{2,1,0:T(8,128)(2,1)} %collective-permute-done.20), channel_id=1, source_target_pairs={{0,4},{4,0},{1,5},{5,1},{2,6},{6,2},{3,7},{7,3},{8,12},{12,8},{9,1... | collective-permute-start | bytes 4478984 | tf_op jit(solution)/shard_map/ppermute | solution.py:73
  218.0 247.3 %collective-permute-start.14 = (bf16[2,128,1152]{2,1,0:T(8,128)(2,1)}, bf16[2,128,1152]{2,1,0:T(8,128)(2,1)}, u32[]{:S(2)}, u32[]{:S(2)}) collective-permute-start(bf16[2,128,1152]{2,1,0:T(8,128)(2,1)} %pad_maximum_fusion.6), channel_id=1, source_target_pairs={{0,1},{1,0},{2,3},{3,2},{4,5},{5,4},{6,7},{7,6},{8,9},{9,8},{10,11... | collective-permute-start | bytes 1769480 | tf_op jit(solution)/shard_map/ppermute | solution.py:73
  588.8 250.0 %collective-permute-start.55 = (bf16[2,144,1728]{2,1,0:T(8,128)(2,1)}, bf16[2,144,1728]{2,1,0:T(8,128)(2,1)}, u32[]{:S(2)}, u32[]{:S(2)}) collective-permute-start(bf16[2,144,1728]{2,1,0:T(8,128)(2,1)} %get-tuple-element.302), channel_id=1, source_target_pairs={{0,4},{4,0},{1,5},{5,1},{2,6},{6,2},{3,7},{7,3},{8,12},{12,8},{9,1... | collective-permute-start | bytes 2985992 | tf_op jit(solution)/shard_map/ppermute | solution.py:73
  590.8 190.9 %collective-permute-start.53 = (bf16[2,144,1728]{2,1,0:T(8,128)(2,1)}, bf16[2,144,1728]{2,1,0:T(8,128)(2,1)}, u32[]{:S(2)}, u32[]{:S(2)}) collective-permute-start(bf16[2,144,1728]{2,1,0:T(8,128)(2,1)} %get-tuple-element.301), channel_id=1, source_target_pairs={{0,4},{4,0},{1,5},{5,1},{2,6},{6,2},{3,7},{7,3},{8,12},{12,8},{9,1... | collective-permute-start | bytes 2985992 | tf_op jit(solution)/shard_map/ppermute | solution.py:73
  590.9 119.4 %collective-permute-start.49 = (bf16[2,144,1728]{2,1,0:T(8,128)(2,1)}, bf16[2,144,1728]{2,1,0:T(8,128)(2,1)}, u32[]{:S(2)}, u32[]{:S(2)}) collective-permute-start(bf16[2,144,1728]{2,1,0:T(8,128)(2,1)} %get-tuple-element.299), channel_id=1, source_target_pairs={{0,4},{4,0},{1,5},{5,1},{2,6},{6,2},{3,7},{7,3},{8,12},{12,8},{9,1... | collective-permute-start | bytes 2985992 | tf_op jit(solution)/shard_map/ppermute | solution.py:73
  596.8 100.9 %collective-permute-start.58 = (bf16[1,144,1728]{2,1,0:T(8,128)(2,1)}, bf16[1,144,1728]{2,1,0:T(8,128)(2,1)}, u32[]{:S(2)}, u32[]{:S(2)}) collective-permute-start(bf16[1,144,1728]{2,1,0:T(8,128)(2,1)} %get-tuple-element.308), channel_id=1, source_target_pairs={{0,4},{4,0},{1,5},{5,1},{2,6},{6,2},{3,7},{7,3},{8,12},{12,8},{9,1... | collective-permute-start | bytes 1493000 | tf_op jit(solution)/shard_map/ppermute | solution.py:73
  596.9 83.5 %collective-permute-start.56 = (bf16[1,144,1728]{2,1,0:T(8,128)(2,1)S(1)}, bf16[1,144,1728]{2,1,0:T(8,128)(2,1)S(1)}, u32[]{:S(2)}, u32[]{:S(2)}) collective-permute-start(bf16[1,144,1728]{2,1,0:T(8,128)(2,1)S(1)} %get-tuple-element.305), channel_id=1, source_target_pairs={{0,4},{4,0},{1,5},{5,1},{2,6},{6,2},{3,7},{7,3},{8,12},{12,8},{9,1... | collective-permute-start | bytes 1493000 | tf_op jit(solution)/shard_map/ppermute | solution.py:73
  713.0 38.5 %collective-permute-start.51 = (bf16[2,144,1728]{2,1,0:T(8,128)(2,1)}, bf16[2,144,1728]{2,1,0:T(8,128)(2,1)}, u32[]{:S(2)}, u32[]{:S(2)}) collective-permute-start(bf16[2,144,1728]{2,1,0:T(8,128)(2,1)} %get-tuple-element.300), channel_id=1, source_target_pairs={{0,4},{4,0},{1,5},{5,1},{2,6},{6,2},{3,7},{7,3},{8,12},{12,8},{9,1... | collective-permute-start | bytes 2985992 | tf_op jit(solution)/shard_map/ppermute | solution.py:73
  720.4 36.6 %collective-permute-start.62 = (bf16[1,144,1728]{2,1,0:T(8,128)(2,1)}, bf16[1,144,1728]{2,1,0:T(8,128)(2,1)}, u32[]{:S(2)}, u32[]{:S(2)}) collective-permute-start(bf16[1,144,1728]{2,1,0:T(8,128)(2,1)} %get-tuple-element.306), channel_id=1, source_target_pairs={{0,4},{4,0},{1,5},{5,1},{2,6},{6,2},{3,7},{7,3},{8,12},{12,8},{9,1... | collective-permute-start | bytes 1493000 | tf_op jit(solution)/shard_map/ppermute | solution.py:73
  723.2 31.7 %collective-permute-start.50 = (bf16[2,144,1728]{2,1,0:T(8,128)(2,1)}, bf16[2,144,1728]{2,1,0:T(8,128)(2,1)}, u32[]{:S(2)}, u32[]{:S(2)}) collective-permute-start(bf16[2,144,1728]{2,1,0:T(8,128)(2,1)} %add_convert_fusion.2), channel_id=1, source_target_pairs={{0,8},{8,24},{24,16},{16,0},{1,9},{9,25},{25,17},{17,1},{2,10},{10... | collective-permute-start | bytes 2985992 | tf_op jit(solution)/shard_map/ppermute | solution.py:134
  763.6 28.9 %collective-permute-start.52 = (bf16[2,144,1728]{2,1,0:T(8,128)(2,1)S(1)}, bf16[2,144,1728]{2,1,0:T(8,128)(2,1)S(1)}, u32[]{:S(2)}, u32[]{:S(2)}) collective-permute-start(bf16[2,144,1728]{2,1,0:T(8,128)(2,1)S(1)} %add_convert_fusion.1), channel_id=1, source_target_pairs={{0,8},{8,24},{24,16},{16,0},{1,9},{9,25},{25,17},{17,1},{2,10},{10... | collective-permute-start | bytes 2985992 | tf_op jit(solution)/shard_map/ppermute | solution.py:134
  771.4 29.2 %collective-permute-start.33 = (bf16[128,1152]{1,0:T(8,128)(2,1)S(1)}, bf16[128,1152]{1,0:T(8,128)(2,1)S(1)}, u32[]{:S(2)}, u32[]{:S(2)}) collective-permute-start(bf16[128,1152]{1,0:T(8,128)(2,1)S(1)} %fusion.67), channel_id=1, source_target_pairs={{0,2},{2,0},{1,3},{3,1},{4,6},{6,4},{5,7},{7,5},{8,10},{10,8},{9,1... | collective-permute-start | bytes 884744 | tf_op jit(solution)/shard_map/ppermute | solution.py:73
  796.6 42.2 %collective-permute-start.54 = (bf16[2,144,1728]{2,1,0:T(8,128)(2,1)}, bf16[2,144,1728]{2,1,0:T(8,128)(2,1)}, u32[]{:S(2)}, u32[]{:S(2)}) collective-permute-start(bf16[2,144,1728]{2,1,0:T(8,128)(2,1)} %add_convert_fusion), channel_id=1, source_target_pairs={{0,8},{8,24},{24,16},{16,0},{1,9},{9,25},{25,17},{17,1},{2,10},{10... | collective-permute-start | bytes 2985992 | tf_op jit(solution)/shard_map/ppermute | solution.py:134
  838.7 19.0 %collective-permute-start.45 = (bf16[4,361,256]{2,0,1:T(4,128)(2,1)S(1)}, bf16[4,361,256]{2,0,1:T(4,128)(2,1)S(1)}, u32[]{:S(2)}, u32[]{:S(2)}) collective-permute-start(bf16[4,361,256]{2,0,1:T(4,128)(2,1)S(1)} %copy.586), channel_id=1, source_target_pairs={{0,4},{4,0},{1,5},{5,1},{2,6},{6,2},{3,7},{7,3},{8,12},{12,8},{9,1... | collective-permute-start | bytes 2217992 | tf_op jit(solution)/shard_map/ppermute | solution.py:73
  858.0 19.8 %collective-permute-start.47 = (bf16[361,256]{1,0:T(8,128)(2,1)S(1)}, bf16[361,256]{1,0:T(8,128)(2,1)S(1)}, u32[]{:S(2)}, u32[]{:S(2)}) collective-permute-start(bf16[361,256]{1,0:T(8,128)(2,1)S(1)} %get-tuple-element.315), channel_id=1, source_target_pairs={{0,16},{8,24},{16,0},{24,8},{1,17},{9,25},{17,1},{25,9},{2,18},{10... | collective-permute-start | bytes 554504 | tf_op jit(solution)/shard_map/ppermute | solution.py:73
  (153 other events, 1667.9 us)

commit v2 on v1

v2 whole, which is shorter than its diff:
```python
import functools

import jax
import jax.numpy as jnp
import numpy as np
from jax import lax
from jax.experimental import pallas as pl
from jax.experimental.pallas import tpu as pltpu
from jax.sharding import Mesh, PartitionSpec as P

HD = 256
SEQ = 2048
ADAM_STEP = 4


EPS = 1e-06
THETA = 1000000.0
LEARN = 0.02
BETA_ONE = 0.9
BETA_TWO = 0.95
ADAM_EPS = 1e-08
DECAY = 0.1
GELU_COEF = 0.7978845608028654
GELU_CUBE = 0.044715
NEG_FILL = -1e30

bf = jnp.bfloat16
fl = jnp.float32
DP = ("z", "y")


def rms_scale(values):
    return lax.rsqrt(jnp.mean(values * values, axis=-1, keepdims=True) + EPS)


def norm_back(values, scale, factor, incoming):
    scaled = incoming * factor
    return scale * (
        scaled - values * (scale * scale) * jnp.mean(scaled * values, axis=-1, keepdims=True)
    )


def rotate_half(values):
    middle = values.shape[-1] // 2
    return jnp.concatenate([-values[..., middle:], values[..., :middle]], axis=-1)


def rope_tables(position, width):
    middle = width // 2
    freqs = THETA ** (-2.0 * jnp.arange(middle, dtype=jnp.float32) / width)
    angle = position.astype(jnp.float32)[:, None] * freqs[None, :]
    cosine = jnp.concatenate([jnp.cos(angle), jnp.cos(angle)], axis=-1)
    sine = jnp.concatenate([jnp.sin(angle), jnp.sin(angle)], axis=-1)
    return (cosine, sine)


def gelu_parts(values):
    inner = GELU_COEF * (values + GELU_CUBE * values * values * values)
    tanh_val = jnp.tanh(inner)
    value = 0.5 * values * (1.0 + tanh_val)
    slope = 0.5 * (1.0 + tanh_val) + 0.5 * values * (1.0 - tanh_val * tanh_val) * GELU_COEF * (
        1.0 + 3.0 * GELU_CUBE * values * values
    )
    return (value, slope)


def adam_update(weight, mom, var, grad, decay):
    mom_new = BETA_ONE * mom + (1.0 - BETA_ONE) * grad
    var_new = BETA_TWO * var + (1.0 - BETA_TWO) * grad * grad
    fix_one = 1.0 - BETA_ONE**ADAM_STEP
    fix_two = 1.0 - BETA_TWO**ADAM_STEP
    direction = mom_new / fix_one / (jnp.sqrt(var_new / fix_two) + ADAM_EPS)
    return (weight - LEARN * (direction + decay * weight), mom_new, var_new)


def rotated(value, axis, by):
    size = lax.axis_size(axis)
    return lax.ppermute(value, axis, [(i, (i + by) % size) for i in range(size)])


def shifted(value, by):
    size = lax.axis_size(DP)
    return lax.ppermute(
        value, DP, [(i, i + by) for i in range(size) if 0 <= i + by < size]
    )


def pick(value, index):
    return lax.dynamic_index_in_dim(value, index, 0, keepdims=False)


def gather_axis(value, axis):
    size = lax.axis_size(axis)
    me = lax.axis_index(axis)
    if size == 2:
        other = rotated(value, axis, 1)
        return jnp.stack([jnp.where(me == 0, value, other), jnp.where(me == 0, other, value)])
    whole = jnp.zeros((size,) + value.shape, value.dtype)
    whole = lax.dynamic_update_index_in_dim(whole, value, me, 0)
    for by in range(1, size):
        whole = lax.dynamic_update_index_in_dim(
            whole, rotated(value, axis, by), (me - by) % size, 0
        )
    return whole


def scatter_axis(pieces, axis):
    size = lax.axis_size(axis)
    me = lax.axis_index(axis)
    total = pick(pieces, me).astype(fl)
    for by in range(1, size):
        sent = pick(pieces, (me + by) % size).astype(bf)
        total = total + rotated(sent, axis, by).astype(fl)
    return total


def scatter_model(partial):
    xs, cs = lax.axis_size("x"), lax.axis_size("c")
    rows, width = partial.shape
    view = partial.reshape(xs, cs, rows // (xs * cs), width)
    half = scatter_axis(view.swapaxes(0, 1), "c")
    return scatter_axis(half, "x")


def gather_model(part):
    both = gather_axis(part, "x")
    four = gather_axis(both, "c")
    four = four.swapaxes(0, 1)
    return four.reshape((-1,) + part.shape[1:])


def ring_index(index, size):
    return index ^ (index >> 1) if size == 4 else index


def ring_step(value):
    size = lax.axis_size("z")
    pairs = [(ring_index(i, size), ring_index((i + 1) % size, size)) for i in range(size)]
    return lax.ppermute(value, "z", pairs)


def ring_source(back):
    size = lax.axis_size("z")
    place = ring_index(lax.axis_index("z"), size)
    return ring_index((place - back + size) % size, size)


def after(value, *others):
    return lax.optimization_barrier((value,) + others)[0]


def over_y(value):
    return [rotated(value, "y", by) for by in range(1, lax.axis_size("y"))]


def in_order(blocks):
    zs, ys = lax.axis_size("z"), lax.axis_size("y")
    me = lax.axis_index("y")
    whole = jnp.zeros((zs * ys,) + blocks[0][0].shape, blocks[0][0].dtype)
    for step, row in enumerate(blocks):
        source = ring_source(step)
        for by, piece in enumerate(row):
            whole = lax.dynamic_update_index_in_dim(
                whole, piece, source * ys + (me - by) % ys, 0
            )
    return whole


TILE = 256
NOMINAL = pl.CostEstimate(flops=1, bytes_accessed=1, transcendentals=0)


def _columns(block, index, valid):
    at = index * TILE + lax.broadcasted_iota(jnp.int32, block.shape, 1)
    return jnp.where(at < valid, block, jnp.zeros_like(block))


def _flat(block):
    return block.reshape(-1, block.shape[-1])


def _hidden_kernel(valid, mid_ref, w_ref, hid_ref, gate_ref, up_ref):
    mid = mid_ref[...]
    gate = jnp.dot(mid, _flat(w_ref[:, 0]), preferred_element_type=fl)
    up = jnp.dot(mid, _flat(w_ref[:, 1]), preferred_element_type=fl)
    value, slope = gelu_parts(gate)
    hid_ref[...] = (value * up).astype(bf)
    gate_ref[...] = (up * slope).astype(bf)
    up_ref[...] = value.astype(bf)


def _down_kernel(valid, hid_ref, down_ref, out_ref):
    index = pl.program_id(0)

    def add(hid, down):
        part = lax.dot_general(hid, down, (((1,), (1,)), ((), ())), preferred_element_type=fl)

        @pl.when(index == 0)
        def _():
            out_ref[...] = part

        @pl.when(index > 0)
        def _():
            out_ref[...] += part

    last = index == pl.num_programs(0) - 1

    @pl.when(jnp.logical_not(last))
    def _():
        add(hid_ref[...], _flat(down_ref[:, 0]))

    @pl.when(last)
    def _():
        add(_columns(hid_ref[...], index, valid), _columns(_flat(down_ref[:, 0]), index, valid))


def _backward_kernel(valid, ffn_ref, gate_ref, up_ref, w_ref, down_ref, mid_ref, ggate_ref, gup_ref):
    index = pl.program_id(0)
    grad = jnp.dot(ffn_ref[...], _flat(down_ref[:, 0]), preferred_element_type=fl)
    ggate = (grad * gate_ref[...].astype(fl)).astype(bf)
    gup = (grad * up_ref[...].astype(fl)).astype(bf)
    ggate_ref[...] = ggate
    gup_ref[...] = gup

    def add(one, two, w_one, w_two):
        dims = (((1,), (1,)), ((), ()))
        part = lax.dot_general(one, w_one, dims, preferred_element_type=fl)
        part = part + lax.dot_general(two, w_two, dims, preferred_element_type=fl)

        @pl.when(index == 0)
        def _():
            mid_ref[...] = part

        @pl.when(index > 0)
        def _():
            mid_ref[...] += part

    last = index == pl.num_programs(0) - 1
    w_one, w_two = _flat(w_ref[:, 0]), _flat(w_ref[:, 1])

    @pl.when(jnp.logical_not(last))
    def _():
        add(ggate, gup, w_one, w_two)

    @pl.when(last)
    def _():
        add(
            _columns(ggate, index, valid),
            _columns(gup, index, valid),
            _columns(w_one, index, valid),
            _columns(w_two, index, valid),
        )


def _grads_kernel(pairs, left_ref, *refs):
    turned = refs[-1]

    @pl.when(pl.program_id(0) == 0)
    def _():
        turned[...] = left_ref[...].T

    for right_ref, out_ref in zip(refs[:pairs], refs[pairs : 2 * pairs]):
        grads = jnp.dot(turned[...], right_ref[...], preferred_element_type=fl).astype(bf)
        out_ref[...] = grads.reshape(out_ref.shape)


def grads_call(left, rights, pieces, name):
    rows, depth = left.shape
    units = rights[0].shape[1]
    split = pieces if depth // pieces % 16 == 0 else 1
    shape = (split, depth // split, units)
    column = pl.BlockSpec((rows, TILE), lambda j: (0, j))
    out = pl.BlockSpec(shape[:2] + (TILE,), lambda j: (0, 0, j))
    results = pl.pallas_call(
        functools.partial(_grads_kernel, len(rights)),
        out_shape=[jax.ShapeDtypeStruct(shape, bf)] * len(rights),
        grid=(pl.cdiv(units, TILE),),
        in_specs=[pl.BlockSpec((rows, depth), lambda j: (0, 0))] + [column] * len(rights),
        out_specs=[out] * len(rights),
        scratch_shapes=[pltpu.VMEM((depth, rows), bf)],
        compiler_params=pltpu.CompilerParams(
            dimension_semantics=("arbitrary",), vmem_limit_bytes=40 * 1024 * 1024
        ),
        cost_estimate=NOMINAL,
        name=name,
    )(left, *rights)
    return [result.reshape(pieces, depth // pieces, units) for result in results]


def ffn_call(kernel, name, rows, lefts, weights, tiles_in, total, tiles_out):
    units = weights[0].shape[-1]
    depth = weights[0].shape[0] * weights[0].shape[2]
    kinds = sum(w.shape[1] for w in weights)
    column = pl.BlockSpec((rows, TILE), lambda j: (0, j))
    whole = pl.BlockSpec((rows, depth), lambda j: (0, 0))
    tile = jax.ShapeDtypeStruct((rows, units), bf)
    return pl.pallas_call(
        functools.partial(kernel, units),
        out_shape=[jax.ShapeDtypeStruct((rows, depth), fl)] * total + [tile] * tiles_out,
        grid=(pl.cdiv(units, TILE),),
        in_specs=[whole] * len(lefts)
        + [column] * len(tiles_in)
        + [pl.BlockSpec(w.shape[:3] + (TILE,), lambda j: (0, 0, 0, j)) for w in weights],
        out_specs=[whole] * total + [column] * tiles_out,
        compiler_params=pltpu.CompilerParams(
            dimension_semantics=("arbitrary",), vmem_limit_bytes=40 * 1024 * 1024
        ),
        cost_estimate=NOMINAL,
        name=name,
    )(*lefts, *tiles_in, *weights)


HALVES = 2


def row_call(kernel, name, rows, by_rows, whole, out_rows, out_whole=(), scratch=()):
    step = rows // HALVES

    def cut(shape):
        return pl.BlockSpec((step,) + shape[1:], lambda i: (i, 0))

    def kept(shape):
        return pl.BlockSpec(shape, lambda i: (0,) * len(shape))

    return pl.pallas_call(
        kernel,
        out_shape=[jax.ShapeDtypeStruct(*item) for item in list(out_rows) + list(out_whole)],
        grid=(HALVES,),
        in_specs=[cut(item.shape) for item in by_rows] + [kept(item.shape) for item in whole],
        out_specs=[cut(item[0]) for item in out_rows] + [kept(item[0]) for item in out_whole],
        scratch_shapes=scratch,
        compiler_params=pltpu.CompilerParams(
            dimension_semantics=("arbitrary",), vmem_limit_bytes=48 * 1024 * 1024
        ),
        cost_estimate=NOMINAL,
        name=name,
    )(*by_rows, *whole)


def _project_kernel(
    x_ref,
    cos_ref,
    sin_ref,
    gain_ref,
    head_ref,
    query_ref,
    keyval_ref,
    normed_ref,
    scale_ref,
    qraw_ref,
    qscale_ref,
    qrot_ref,
    kraw_ref,
    kscale_ref,
    kv_ref,
):
    width = qraw_ref.shape[1]
    values = x_ref[...]
    scale = rms_scale(values)
    scale_ref[...] = scale
    normed = (values * scale * gain_ref[...]).astype(bf)
    normed_ref[...] = normed
    cosine, sine = cos_ref[...], sin_ref[...]

    def turned(raw, scale, factor):
        norm = raw * scale * factor
        return (norm * cosine + rotate_half(norm) * sine).astype(bf)

    raw = jnp.dot(normed, query_ref[...], preferred_element_type=fl)
    scale = rms_scale(raw)
    qraw_ref[...] = raw
    qscale_ref[...] = scale
    qrot_ref[...] = turned(raw, scale, head_ref[0:1])
    raw = jnp.dot(normed, keyval_ref[...], preferred_element_type=fl)
    key = raw[:, :width]
    scale = rms_scale(key)
    kraw_ref[...] = key
    kscale_ref[...] = scale
    kv_ref[:, :width] = turned(key, scale, head_ref[1:2])
    kv_ref[:, width:] = raw[:, width:].astype(bf)


ACROSS = (((1,), (1,)), ((), ()))


def _masked_scores(query, keys, low, high, factor):
    scores = lax.dot_general(query, keys, ACROSS, preferred_element_type=fl) * factor
    at = lax.broadcasted_iota(jnp.int32, scores.shape, 1)
    return jnp.where((at >= low) & (at <= high), scores, NEG_FILL)


def _attend_kernel(
    factor, query_ref, low_ref, high_ref, window_ref, out_ref, att_ref, log_ref, part_ref
):
    width = query_ref.shape[1]
    masked = _masked_scores(
        query_ref[...], window_ref[:, :width], low_ref[...], high_ref[...], factor
    )
    top = jnp.max(masked, axis=-1, keepdims=True)
    powers = jnp.exp(masked - top)
    total = jnp.sum(powers, axis=-1, keepdims=True)
    log_ref[...] = top + jnp.log(total)
    probs = (powers * (1.0 / total)).astype(bf)
    attended = jnp.dot(probs, window_ref[:, width:], preferred_element_type=fl).astype(bf)
    att_ref[...] = attended
    part_ref[...] = lax.dot_general(attended, out_ref[...], ACROSS, preferred_element_type=fl)


def _attend_back_kernel(
    factor,
    grad_ref,
    query_ref,
    low_ref,
    high_ref,
    log_ref,
    att_ref,
    qraw_ref,
    qscale_ref,
    cos_ref,
    sin_ref,
    head_ref,
    window_ref,
    out_ref,
    lowq_ref,
    gqin_ref,
    part_ref,
    gkv_ref,
    ghead_ref,
    turned,
):
    width = query_ref.shape[1]
    keys, values = window_ref[:, :width], window_ref[:, width:]
    query = query_ref[...]
    grad_att = jnp.dot(grad_ref[...], out_ref[...], preferred_element_type=fl).astype(bf)
    delta = jnp.sum(
        grad_att.astype(fl) * att_ref[...].astype(fl), axis=-1, keepdims=True
    )
    masked = _masked_scores(query, keys, low_ref[...], high_ref[...], factor)
    probs = jnp.exp(masked - log_ref[...])
    grad_probs = lax.dot_general(grad_att, values, ACROSS, preferred_element_type=fl)
    grad_scores = (probs * (grad_probs - delta) * factor).astype(bf)
    grad_q = jnp.dot(grad_scores, keys, preferred_element_type=fl)
    grad_k = jnp.dot(query.T, grad_scores, preferred_element_type=fl)
    grad_v = jnp.dot(grad_att.T, probs.astype(bf), preferred_element_type=fl)
    back = grad_q * cos_ref[...] - rotate_half(grad_q * sin_ref[...])
    raw, scale = qraw_ref[...], qscale_ref[...]
    gqin = norm_back(raw, scale, head_ref[0:1], back).astype(bf)
    gqin_ref[...] = gqin
    part_ref[...] = lax.dot_general(gqin, lowq_ref[...], ACROSS, preferred_element_type=fl)
    ghead = jnp.sum(back * raw * scale, axis=0, keepdims=True)
    first = pl.program_id(0) == 0

    @pl.when(first)
    def _():
        turned[:width] = grad_k
        turned[width:] = grad_v
        ghead_ref[...] = ghead

    @pl.when(jnp.logical_not(first))
    def _():
        turned[:width] += grad_k
        turned[width:] += grad_v
        ghead_ref[...] += ghead

    @pl.when(pl.program_id(0) == pl.num_programs(0) - 1)
    def _():
        gkv_ref[...] = turned[...].astype(bf).T


def on_device(
    block_in,
    out_grad,
    segment_ids,
    w_query,
    w_keyval,
    w_out,
    w_gateup,
    w_down,
    gain_layers,
    gain_heads,
    mom_query,
    var_query,
    mom_keyval,
    var_keyval,
    mom_out,
    var_out,
    mom_gateup,
    var_gateup,
    mom_down,
    var_down,
    mom_layers,
    var_layers,
    mom_heads,
    var_heads,
):
    zs, ys = lax.axis_size("z"), lax.axis_size("y")
    xs, cs = lax.axis_size("x"), lax.axis_size("c")
    dps, mps = zs * ys, xs * cs
    model = lax.axis_index("x") * cs + lax.axis_index("c")
    device = lax.axis_index("z") * ys + lax.axis_index("y")
    width = HD
    rows, depth = block_in.shape
    quarter = rows // mps
    factor = width ** (-0.5)
    norm_factor = float(rows * dps) ** (-0.5)
    drows = w_query.shape[0]
    krows = w_keyval.shape[0]
    gcols, hcols = gain_layers.shape[1], gain_heads.shape[1]

    kpad = -(-krows // 16) * 16
    small = jnp.concatenate([gain_layers.reshape(-1), gain_heads.reshape(-1)]).astype(bf)
    small = jnp.pad(small, (0, width - small.shape[0])).reshape(1, width)
    fill = jnp.zeros((kpad - krows, width), bf)
    pack = jnp.concatenate(
        [
            w_query.astype(bf),
            w_keyval[:, :width].astype(bf),
            fill,
            w_keyval[:, width:].astype(bf),
            fill,
            jnp.pad(small, ((0, 15), (0, 0))),
        ],
        axis=0,
    )
    by_z = gather_axis(pack, "z")
    by_dp = gather_axis(by_z, "y").swapaxes(0, 1).reshape((dps,) + pack.shape)
    low_query = by_dp[:, :drows].reshape(depth, width)
    kv_mine = by_dp[:, drows:]

    gateup0, down0 = w_gateup.astype(bf), w_down.T.astype(bf)
    gateup1 = ring_step(after(gateup0, by_z))
    gateup0_y = over_y(after(gateup0, by_dp))
    gateup2 = ring_step(gateup1)
    gateup1_y = over_y(after(gateup1, *gateup0_y))
    gateup3 = ring_step(gateup2)
    down_y = over_y(after(down0, *gateup1_y))

    kv_all = gather_axis(gather_axis(after(kv_mine, gateup1), "x"), "c")
    kv_all = after(kv_all, gateup2, *gateup0_y)
    lanes = np.arange(cs * xs * dps * kpad).reshape(cs, xs, dps, kpad)
    core, xx, dd, rr = np.unravel_index(lanes.reshape(-1), lanes.shape)
    owner = np.where(rr < krows, (dd * mps + xx * cs + core) * krows + rr, -1)
    depth_index = jnp.arange(depth, dtype=jnp.int32)
    sorter = (depth_index[:, None] == jnp.asarray(owner, jnp.int32)[None, :]).astype(bf)
    kv_pad = jnp.concatenate(
        [
            kv_all[:, :, :, :kpad].reshape(-1, width),
            kv_all[:, :, :, kpad : 2 * kpad].reshape(-1, width),
        ],
        axis=1,
    )
    low_keyval = jnp.dot(sorter, kv_pad, preferred_element_type=fl).astype(bf)
    low_keyval = after(low_keyval, gateup3, *gateup1_y)
    mine = np.arange(dps * kpad)
    owner = (mine // kpad) * mps * krows + mine % kpad
    owner = jnp.asarray(owner, jnp.int32) + model * krows
    chooser = (depth_index[:, None] == owner[None, :]) & jnp.asarray(mine % kpad < krows)[None, :]
    gains = kv_all[:, :, :, 2 * kpad].astype(fl)
    gain_scale = 1.0 + gains[:, :, :, : 4 * gcols].reshape(cs, xs, dps, 4, gcols).transpose(
        3, 2, 1, 0, 4
    ).reshape(4, depth)
    head_scale = 1.0 + gains[:, :, :, 4 * gcols : 4 * gcols + 2 * hcols].reshape(
        cs, xs, dps, 2, hcols
    ).transpose(3, 2, 1, 0, 4).reshape(2, width)

    margin = SEQ // 2
    first_row = device * rows
    shifted_first = first_row + margin
    seq_start = shifted_first // SEQ * SEQ
    span = SEQ // rows
    position = shifted_first + jnp.arange(rows, dtype=jnp.int32)
    cosine, sine = rope_tables(position % SEQ, width)

    def part_rows(values):
        return lax.dynamic_slice_in_dim(values, model * quarter, quarter, 0)

    (
        normed_in,
        scale_in,
        query_raw,
        scale_query,
        query_rot,
        key_raw,
        scale_key,
        keyval_low,
    ) = row_call(
        _project_kernel,
        "project",
        rows,
        [block_in, cosine, sine],
        [gain_scale[0:1], head_scale, low_query, low_keyval],
        [
            ((rows, depth), bf),
            ((rows, 1), fl),
            ((rows, width), fl),
            ((rows, 1), fl),
            ((rows, width), bf),
            ((rows, width), fl),
            ((rows, 1), fl),
            ((rows, 2 * width), bf),
        ],
    )
    sent_kv = after(part_rows(keyval_low), *down_y)
    earlier = jnp.stack([shifted(sent_kv, by) for by in range(span - 1, 0, -1)])
    out_by_z = gather_axis(after(w_out.T.astype(bf), sent_kv), "z")
    low_out = gather_axis(out_by_z, "y").swapaxes(0, 1).reshape(depth, width)
    down0 = after(jnp.stack([down0] + down_y), earlier, out_by_z)
    down1 = ring_step(down0)
    gateup2_y = over_y(after(gateup2, earlier, low_out))
    four = gather_axis(gather_axis(earlier, "x"), "c")
    earlier = four.transpose(2, 1, 0, 3, 4).reshape((span - 1) * rows, 2 * width)
    earlier = after(earlier, down1, *gateup2_y)
    window = jnp.concatenate([earlier, keyval_low], axis=0)
    reach = span * rows
    window_first = first_row + rows - reach
    seg_query = lax.dynamic_slice_in_dim(segment_ids, first_row, rows, 0)
    doc_first = jnp.sum(
        (segment_ids[None, :] < seg_query[:, None]).astype(jnp.int32), axis=1, keepdims=True
    )
    run_first = jnp.maximum(doc_first, seq_start - margin) - window_first
    run_last = jnp.arange(rows, dtype=jnp.int32)[:, None] + (reach - rows)
    attended, log_total, attn_part = row_call(
        functools.partial(_attend_kernel, factor),
        "attend",
        rows,
        [query_rot, run_first, run_last],
        [window, low_out],
        [((rows, width), bf), ((rows, 1), fl), ((rows, depth), fl)],
    )
    down2 = ring_step(down1)
    gateup3_y = over_y(after(gateup3, *gateup2_y))

    in_part, scale_in_part = part_rows(block_in), part_rows(scale_in)
    grad_part = part_rows(out_grad)
    attn_proj = after(scatter_model(attn_part), down2, *gateup3_y)
    down3 = ring_step(down2)
    scale_attn = rms_scale(attn_proj)
    resid = in_part + attn_proj * scale_attn * gain_scale[1]
    scale_mid = rms_scale(resid)
    normed_mid = gather_model((resid * scale_mid * gain_scale[2]).astype(bf))
    low_gateup = in_order(
        [
            [gateup0] + gateup0_y,
            [gateup1] + gateup1_y,
            [gateup2] + gateup2_y,
            [gateup3] + gateup3_y,
        ]
    )
    low_down = in_order([[block[by] for by in range(ys)] for block in (down0, down1, down2, down3)])
    low_down = low_down[:, None]
    if drows % 16:
        low_gateup = low_gateup.swapaxes(0, 1).reshape((1, 2, depth, -1))
        low_down = low_down.reshape((1, 1, depth, -1))
    hidden, gate_factor, up_factor = ffn_call(
        _hidden_kernel, "ffn_hidden", rows, [normed_mid], [low_gateup], [], 0, 3
    )
    (ffn_part,) = ffn_call(_down_kernel, "ffn_down", rows, [], [low_down], [hidden], 1, 0)
    ffn_proj = scatter_model(ffn_part)
    scale_ffn = rms_scale(ffn_proj)
    out_part = resid + ffn_proj * scale_ffn * gain_scale[3]
    grad_ffn = gather_model(norm_back(ffn_proj, scale_ffn, gain_scale[3], grad_part).astype(bf))
    (grad_down,) = grads_call(grad_ffn, [hidden], dps, "down_grads")
    grad_down = grad_down.reshape((zs, ys) + grad_down.shape[1:])
    sum_down1 = ring_step(pick(grad_down, ring_source(1)))
    grad_ffn = after(grad_ffn, grad_down)
    mid_part, grad_gate, grad_up = ffn_call(
        _backward_kernel,
        "ffn_backward",
        rows,
        [grad_ffn],
        [low_gateup, low_down],
        [gate_factor, up_factor],
        1,
        2,
    )
    grads_gateup = grads_call(normed_mid, [grad_gate, grad_up], dps, "gateup_grads")

    def gateup_piece(target, by):
        index = ring_source(target) * ys + (lax.axis_index("y") + by) % ys
        return jnp.stack([pick(item, index) for item in grads_gateup])

    def gateup_over_y(target, *others):
        total = gateup_piece(target, 0).astype(fl)
        for by in range(1, ys):
            sent = after(gateup_piece(target, by), *others)
            total = total + rotated(sent, "y", by).astype(fl)
        return total

    def down_add(came, target):
        return came.astype(fl) + pick(grad_down, ring_source(target)).astype(fl)

    gateup_a = gateup_over_y(1)
    gateup_b = gateup_over_y(2, gateup_a)
    gateup_c = gateup_over_y(3, gateup_b)
    gateup_d = gateup_over_y(4, gateup_c)
    sum_down2 = ring_step(down_add(sum_down1, 2).astype(bf))
    sum_down3 = ring_step(down_add(sum_down2, 3).astype(bf))
    grad_mid = after(scatter_model(after(mid_part, sum_down1)), sum_down2)
    block_out = gather_model(after(out_part, grad_mid).astype(bf)).astype(fl)
    grad_resid = grad_part + norm_back(resid, scale_mid, gain_scale[2], grad_mid)
    grad_attn = gather_model(
        norm_back(attn_proj, scale_attn, gain_scale[1], grad_resid).astype(bf)
    )
    grad_attn = after(grad_attn, sum_down3, gateup_a)
    sum_gateup1 = ring_step(after(gateup_a, sum_down3).astype(bf))
    sum_gateup2 = ring_step((sum_gateup1.astype(fl) + gateup_b).astype(bf))
    grad_out = jnp.einsum("td,tc->dc", grad_attn, attended, preferred_element_type=fl)
    grad_qin, normed_part, grad_seq, grad_qhead = row_call(
        functools.partial(_attend_back_kernel, factor),
        "attend_back",
        rows,
        [
            grad_attn,
            query_rot,
            run_first,
            run_last,
            log_total,
            attended,
            query_raw,
            scale_query,
            cosine,
            sine,
        ],
        [head_scale, window, low_out, low_query],
        [((rows, width), bf), ((rows, depth), fl)],
        [((reach, 2 * width), bf), ((1, width), fl)],
        [pltpu.VMEM((2 * width, reach), fl)],
    )
    by_model = grad_seq.reshape(span, xs, cs, quarter, 2 * width).transpose(2, 1, 0, 3, 4)
    by_block = after(scatter_axis(by_model, "c"), sum_gateup1, gateup_b)
    by_block = after(scatter_axis(by_block, "x"), sum_gateup2, gateup_d)
    grad_kpart = by_block[span - 1]
    for by in range(1, span):
        grad_kpart = grad_kpart + shifted(by_block[span - 1 - by].astype(bf), -by).astype(fl)

    sum_gateup3 = after(sum_gateup2.astype(fl) + gateup_c, grad_kpart)
    sum_gateup3 = ring_step(sum_gateup3.astype(bf))
    sum_down = down_add(sum_down3, 4)
    own = lax.axis_index("y")
    sum_down_own = pick(sum_down, own)
    for by in range(1, ys):
        sent = after(pick(sum_down, (own + by) % ys).astype(bf), gateup_d)
        sum_down_own = sum_down_own + rotated(sent, "y", by).astype(fl)
    sum_down = sum_down_own.T

    cos_part, sin_part = part_rows(cosine), part_rows(sine)
    key_part, scale_kpart = part_rows(key_raw), part_rows(scale_key)
    grad_krot = grad_kpart[:, :width]
    key_back = grad_krot * cos_part - rotate_half(grad_krot * sin_part)
    grad_kin = norm_back(key_part, scale_kpart, head_scale[1], key_back)
    grad_kvin = jnp.concatenate([grad_kin, grad_kpart[:, width:]], axis=1).astype(bf)
    keyval_part = jnp.einsum("tc,dc->td", grad_kvin, low_keyval, preferred_element_type=fl)
    normed_mine = jnp.dot(normed_in, chooser.astype(bf), preferred_element_type=fl).astype(bf)
    grad_keyval = jnp.einsum(
        "td,tc->dc", normed_mine, gather_model(grad_kvin), preferred_element_type=fl
    ).reshape(dps, kpad, 2 * width)

    grad_query = jnp.einsum("td,tc->dc", normed_in, grad_qin, preferred_element_type=fl)
    grad_normed = scatter_model(normed_part) + keyval_part
    grad_in_part = grad_resid + norm_back(in_part, scale_in_part, gain_scale[0], grad_normed)
    grad_input = gather_model(grad_in_part.astype(bf)).astype(fl)

    grad_layers = jnp.stack(
        [
            jnp.sum(grad_normed * in_part * scale_in_part, axis=0),
            jnp.sum(grad_resid * attn_proj * scale_attn, axis=0),
            jnp.sum(grad_mid * resid * scale_mid, axis=0),
            jnp.sum(grad_part * ffn_proj * scale_ffn, axis=0),
        ]
    )
    grad_heads = jnp.stack(
        [
            grad_qhead[0],
            jnp.sum(key_back * key_part * scale_kpart, axis=0),
        ]
    )
    grad_small = jnp.concatenate(
        [
            grad_layers.reshape(4, dps, mps, gcols).transpose(1, 2, 0, 3).reshape(dps, mps, -1),
            grad_heads.reshape(2, dps, mps, hcols).transpose(1, 2, 0, 3).reshape(dps, mps, -1),
        ],
        axis=2,
    )
    grad_small = jnp.pad(grad_small, ((0, 0), (0, 0), (0, width - grad_small.shape[2])))
    grad_small = grad_small.reshape(dps, xs, cs, width).transpose(2, 1, 0, 3)
    grad_small = scatter_axis(scatter_axis(grad_small, "c"), "x")
    def scatter_data(pieces):
        pieces = pieces.reshape((zs, ys) + pieces.shape[1:]).swapaxes(0, 1)
        return scatter_axis(scatter_axis(pieces, "y"), "z")

    grad_qo = jnp.concatenate(
        [
            grad_query.reshape(dps, drows, width).astype(bf),
            grad_out.reshape(dps, drows, width).astype(bf),
        ],
        axis=1,
    )
    sums_qo = scatter_data(after(grad_qo, by_block, sum_down_own))
    sum_query, sum_out = sums_qo[:drows], sums_qo[drows:].T
    grad_pack = jnp.concatenate(
        [
            grad_keyval[:, :, :width].astype(bf),
            grad_keyval[:, :, width:].astype(bf),
            jnp.pad(grad_small[:, None].astype(bf), ((0, 0), (0, 15), (0, 0))),
        ],
        axis=1,
    )
    sums_pack = scatter_data(after(grad_pack, sum_gateup3))
    sum_gateup = sum_gateup3.astype(fl) + gateup_d
    sum_keyval = jnp.concatenate([sums_pack[:krows], sums_pack[kpad : kpad + krows]], axis=1)
    sum_small = sums_pack[2 * kpad]
    sum_layers = sum_small[: 4 * gcols].reshape(4, gcols)
    sum_heads = sum_small[4 * gcols : 4 * gcols + 2 * hcols].reshape(2, hcols)

    masters = (w_query, w_keyval, w_out, w_gateup, w_down, gain_layers, gain_heads)
    sums = (sum_query, sum_keyval, sum_out, sum_gateup, sum_down, sum_layers, sum_heads)
    totals = tuple((item * norm_factor for item in sums))
    moms = (mom_query, mom_keyval, mom_out, mom_gateup, mom_down, mom_layers, mom_heads)
    varis = (var_query, var_keyval, var_out, var_gateup, var_down, var_layers, var_heads)
    decays = (DECAY, DECAY, DECAY, DECAY, DECAY, 0.0, 0.0)
    updated = [
        adam_update(master, mom, var, grad, decay)
        for master, mom, var, grad, decay in zip(masters, moms, varis, totals, decays)
    ]
    return (
        (block_out, grad_input)
        + totals
        + tuple(item[0] for item in updated)
        + tuple(item[1] for item in updated)
        + tuple(item[2] for item in updated)
    )


def solution(mesh):
    dps, mps = mesh.shape["dp"], mesh.shape["mp"]
    zs = 4 if dps % 4 == 0 else 1
    cs = 2 if mps % 2 == 0 else 1
    split = Mesh(mesh.devices.reshape(zs, dps // zs, mps // cs, cs), ("z", "y", "x", "c"))
    mp = ("x", "c")
    both = DP + mp
    weights = (
        P(DP, mp),
        P(both, None),
        P(mp, DP),
        P(None, DP, mp),
        P(mp, DP),
        P(None, both),
        P(None, both),
    )
    tokens = P(DP, None)
    states = tuple(spec for spec in weights for _ in range(2))
    in_specs = (tokens, tokens, P()) + weights + states
    out_specs = (tokens, tokens) + weights * 4
    return jax.shard_map(
        on_device, mesh=split, in_specs=in_specs, out_specs=out_specs, check_vma=False
    )
```

time: 899 us -> 519 us (0.58)
  local copies, waits for them, and re-layouts: 355 us -> 57.3 us
  waiting for transfers between devices: 304 us -> 234 us
  Pallas kernels: 0 us -> 59.3 us
  matrix products: 54 us -> 10.3 us
  other arithmetic: 82.4 us -> 60.1 us
  starting transfers between devices: 71.9 us -> 84.7 us
  between operations: 15.1 us -> 3.72 us
    dynamic_update_slice x8 -> x15, local copies, waits for them, and re-layouts: 231 us -> 12.6 us  [in_order(): lax.dynamic_update_index_in_dim(whole, piece, source * ys + (me - by) % y...]
    pallas_call x0 -> x8, Pallas kernels: none -> 59.3 us  [the longest x3 30.4 us: ffn_call(): pl.pallas_call(functools.partial(kernel, units), out_shape=[jax.ShapeDtyp...]
    dot_general x21 -> x3, matrix products: 50.2 us -> 5.54 us  [the longest x1 3.01 us: on_device(): low_keyval = jnp.dot(sorter, kv_pad, preferred_element_type=fl).astype(bf)]
    ppermute x48 -> x54, waiting for transfers between devices: 193 us -> 149 us  [rotated(): lax.ppermute(value, axis, [(i, (i + by) % size) for i in range(size)])]
    ppermute x7 -> x0, local copies, waits for them, and re-layouts: 27.9 us -> none  [the longest x4 15.9 us: rotated(): lax.ppermute(value, axis, [(i, (i + by) % size) for i in range(size)])]
    ppermute x9 -> x12, waiting for transfers between devices: 105 us -> 81.7 us  [ring_step(): return lax.ppermute(value, 'z', pairs)]
    concatenate x10 -> x2, local copies, waits for them, and re-layouts: 17.6 us -> 0.28 us  [the longest x1 0.25 us: on_device(): jnp.concatenate([w_query.astype(bf), w_keyval[:, :width].astype(bf), fill...]
    ppermute x48 -> x54, starting transfers between devices: 41.8 us -> 54.5 us  [rotated(): lax.ppermute(value, axis, [(i, (i + by) % size) for i in range(size)])]
  transfers between devices with their start and end apart: 63 -> 72, of which waited for: 29 -> 37; matrix products, arithmetic and copies ran while one was open for 42% -> 20% of each run, Pallas kernels for 0% -> 8%
where the time goes in v2:
time: 519 us; the launch traced here: 510 us
  waiting for transfers between devices  234 us (45%)
  starting transfers between devices  84.7 us (16%)
  other arithmetic  60.1 us (12%)
  Pallas kernels  59.3 us (11%)
  local copies, waits for them, and re-layouts  57.3 us (11%)
  matrix products  10.3 us (2%)
    ppermute x54, waiting for transfers between devices, rotated(): lax.ppermute(value, axis, [(i, (i + by) % size) for i in range(size)])  149 us
    ppermute x12, waiting for transfers between devices, ring_step(): return lax.ppermute(value, 'z', pairs)  81.7 us
    ppermute x54, starting transfers between devices, rotated(): lax.ppermute(value, axis, [(i, (i + by) % size) for i in range(size)])  54.5 us
    pallas_call x3, Pallas kernels, ffn_call(): pl.pallas_call(functools.partial(kernel, units), out_shape=[jax.ShapeDtyp...  30.4 us
    pallas_call x3, Pallas kernels, row_call(): pl.pallas_call(kernel, out_shape=[jax.ShapeDtypeStruct(*item) for item in...  18.2 us
    ppermute x12, starting transfers between devices, ring_step(): return lax.ppermute(value, 'z', pairs)  15.7 us
    ppermute x6, starting transfers between devices, shifted(): lax.ppermute(value, DP, [(i, i + by) for i in range(size) if 0 <= i + by...  14.5 us
    dynamic_update_slice x15, local copies, waits for them, and re-layouts, in_order(): lax.dynamic_update_index_in_dim(whole, piece, source * ys + (me - by) % y...  12.6 us
  transfers between devices with their start and end apart: 72, of which 37 were waited for; matrix products, arithmetic and copies ran while one was open for 20% of the time, Pallas kernels for 8%

profile of v2, /device:TPU:0, one launch (start us, length us, event | category | flops | bytes accessed | tf_op | source)
XLA Modules:
  0.0 509.6 jit_solution(10621799894801559754)
XLA Ops:
  4.4 5.1 %collective-permute-start.2 = (bf16[256,256]{1,0:T(8,128)(2,1)S(1)}, bf16[256,256]{1,0:T(8,128)(2,1)S(1)}, u32[]{:S(2)}, u32[]{:S(2)}) collective-permute-start(bf16[256,256]{1,0:T(8,128)(2,1)S(1)} %concatenate.43), channel_id=1, source_target_pairs={{0,24},{8,0},{16,8},{24,16},{1,25},{9,1},{17,9},{25,17},{2,26},{10... | collective-permute-start | bytes 393224 | tf_op jit(solution)/shard_map/ppermute | solution.py:78
  23.5 10.6 %collective-permute-done.3 = bf16[4,256,256]{2,1,0:T(8,128)(2,1)S(1)} collective-permute-done((bf16[4,256,256]{2,1,0:T(8,128)(2,1)S(1)}, bf16[4,256,256]{2,1,0:T(8,128)(2,1)S(1)}, u32[]{:S(2)}, u32[]{:S(2)}) %collective-permute-start.3) | collective-permute-done | bytes 524320 | tf_op jit(solution)/shard_map/ppermute | solution.py:78
  35.9 11.5 %collective-permute-done.4 = bf16[2,144,1728]{2,1,0:T(8,128)(2,1)} collective-permute-done((bf16[2,144,1728]{2,1,0:T(8,128)(2,1)}, bf16[2,144,1728]{2,1,0:T(8,128)(2,1)}, u32[]{:S(2)}, u32[]{:S(2)}) %collective-permute-start.4) | collective-permute-done | bytes 995360 | tf_op jit(solution)/shard_map/ppermute | solution.py:139
  49.0 8.9 %collective-permute-done.5 = bf16[8,112,256]{2,1,0:T(8,128)(2,1)S(1)} collective-permute-done((bf16[8,112,256]{2,1,0:T(8,128)(2,1)S(1)}, bf16[8,112,256]{2,1,0:T(8,128)(2,1)S(1)}, u32[]{:S(2)}, u32[]{:S(2)}) %collective-permute-start.5) | collective-permute-done | bytes 458784 | tf_op jit(solution)/shard_map/ppermute | solution.py:78
  62.5 10.3 %collective-permute-done.7 = bf16[2,144,1728]{2,1,0:T(8,128)(2,1)} collective-permute-done((bf16[2,144,1728]{2,1,0:T(8,128)(2,1)}, bf16[2,144,1728]{2,1,0:T(8,128)(2,1)}, u32[]{:S(2)}, u32[]{:S(2)}) %collective-permute-start.7) | collective-permute-done | bytes 995360 | tf_op jit(solution)/shard_map/ppermute | solution.py:139
  88.8 6.9 %collective-permute-done.9 = bf16[2,144,1728]{2,1,0:T(8,128)(2,1)} collective-permute-done((bf16[2,144,1728]{2,1,0:T(8,128)(2,1)}, bf16[2,144,1728]{2,1,0:T(8,128)(2,1)}, u32[]{:S(2)}, u32[]{:S(2)}) %collective-permute-start.9) | collective-permute-done | bytes 995360 | tf_op jit(solution)/shard_map/ppermute | solution.py:139
  124.0 15.1 %collective-permute-done.20 = bf16[2,144,1728]{2,1,0:T(8,128)(2,1)S(1)} collective-permute-done((bf16[2,144,1728]{2,1,0:T(8,128)(2,1)S(1)}, bf16[2,144,1728]{2,1,0:T(8,128)(2,1)S(1)}, u32[]{:S(2)}, u32[]{:S(2)}) %collective-permute-start.20) | collective-permute-done | bytes 995360 | tf_op jit(solution)/shard_map/ppermute | solution.py:139
  144.9 5.5 %attend.1 = (bf16[512,256]{1,0:T(8,128)(2,1)S(1)}, f32[512,1]{1,0:T(8,128)S(1)}, f32[512,1152]{1,0:T(8,128)}) custom-call(bf16[512,256]{1,0:T(8,128)(2,1)S(1)} %get-tuple-element.88.query_ref, s32[512,1]{1,0:T(8,128)S(1)} %copy.122.low_ref, s32[512,1]{1,0:T(8,128)S(1)} %iota_add_fusion.high_ref, ...), custom_call_target="tpu_custom_call" | custom-call | flops 1 | bytes 1 | tf_op jit(solution)/shard_map/attend/pallas_call | solution.py:325
  169.5 6.9 %collective-permute-done.27 = bf16[128,1152]{1,0:T(8,128)(2,1)S(1)} collective-permute-done((bf16[128,1152]{1,0:T(8,128)(2,1)S(1)}, bf16[128,1152]{1,0:T(8,128)(2,1)S(1)}, u32[]{:S(2)}, u32[]{:S(2)}) %collective-permute-start.27) | collective-permute-done | bytes 294944 | tf_op jit(solution)/shard_map/ppermute | solution.py:78
  176.8 5.3 %collective-permute-done.29 = bf16[2,144,1728]{2,1,0:T(8,128)(2,1)S(1)} collective-permute-done((bf16[2,144,1728]{2,1,0:T(8,128)(2,1)S(1)}, bf16[2,144,1728]{2,1,0:T(8,128)(2,1)S(1)}, u32[]{:S(2)}, u32[]{:S(2)}) %collective-permute-start.29) | collective-permute-done | bytes 995360 | tf_op jit(solution)/shard_map/ppermute | solution.py:139
  182.5 10.7 %ffn_hidden.1 = (bf16[512,1728]{1,0:T(8,128)(2,1)S(1)}, bf16[512,1728]{1,0:T(8,128)(2,1)S(1)}, bf16[512,1728]{1,0:T(8,128)(2,1)S(1)}) custom-call(bf16[512,1152]{1,0:T(8,128)(2,1)S(1)} %bitcast.401, bf16[8,2,144,1728]{3,2,1,0:T(8,128)(2,1)} %bitcast_dynamic-update-slice_fusion.w_ref), custom_call_target="tpu_custom_call" | custom-call | flops 1 | bytes 1 | tf_op jit(solution)/shard_map/ffn_hidden/pallas_call | solution.py:297
  194.4 5.8 %ffn_down.1 = f32[512,1152]{1,0:T(8,128)S(1)} custom-call(bf16[512,1728]{1,0:T(8,128)(2,1)S(1)} %get-tuple-element.99.hid_ref.refs_0_, bf16[8,1,144,1728]{3,2,1,0:T(8,128)(2,1)S(1)} %fusion.21.down_ref), custom_call_target="tpu_custom_call" | custom-call | flops 1 | bytes 1 | tf_op jit(solution)/shard_map/ffn_down/pallas_call | solution.py:297
  207.0 6.6 %collective-permute-done.31 = bf16[128,1152]{1,0:T(8,128)(2,1)} collective-permute-done((bf16[128,1152]{1,0:T(8,128)(2,1)}, bf16[128,1152]{1,0:T(8,128)(2,1)}, u32[]{:S(2)}, u32[]{:S(2)}) %collective-permute-start.31) | collective-permute-done | bytes 294944 | tf_op jit(solution)/shard_map/ppermute | solution.py:78
  247.5 13.9 %ffn_backward.1 = (f32[512,1152]{1,0:T(8,128)S(1)}, bf16[512,1728]{1,0:T(8,128)(2,1)S(1)}, bf16[512,1728]{1,0:T(8,128)(2,1)S(1)}) custom-call(bf16[512,1152]{1,0:T(8,128)(2,1)S(1)} %bitcast.400, bf16[512,1728]{1,0:T(8,128)(2,1)S(1)} %copy-done.14, bf16[512,1728]{1,0:T(8,128)(2,1)S(1)} %copy-done.16, ...), custom_call_target="tpu_custom_call" | custom-call | flops 1 | bytes 1 | tf_op jit(solution)/shard_map/ffn_backward/pallas_call | solution.py:297
  261.4 6.6 %gateup_grads.1 = (bf16[8,144,1728]{2,1,0:T(8,128)(2,1)S(1)}, bf16[8,144,1728]{2,1,0:T(8,128)(2,1)S(1)}) custom-call(bf16[512,1152]{1,0:T(8,128)(2,1)S(1)} %bitcast.402, bf16[512,1728]{1,0:T(8,128)(2,1)S(1)} %get-tuple-element.108.refs_0_, bf16[512,1728]{1,0:T(8,128)(2,1)S(1)} %get-tuple-element.109.refs_1_), custom_call_target="tpu_custom_call" | custom-call | flops 1 | bytes 1 | tf_op jit(solution)/shard_map/gateup_grads/pallas_call | solution.py:274
  277.5 19.0 %collective-permute-done.43 = bf16[2,144,1728]{2,1,0:T(8,128)(2,1)S(1)} collective-permute-done((bf16[2,144,1728]{2,1,0:T(8,128)(2,1)S(1)}, bf16[2,144,1728]{2,1,0:T(8,128)(2,1)S(1)}, u32[]{:S(2)}, u32[]{:S(2)}) %collective-permute-start.43) | collective-permute-done | bytes 995360 | tf_op jit(solution)/shard_map/ppermute | solution.py:78
  301.3 17.3 %collective-permute-done.52 = bf16[2,144,1728]{2,1,0:T(8,128)(2,1)S(1)} collective-permute-done((bf16[2,144,1728]{2,1,0:T(8,128)(2,1)S(1)}, bf16[2,144,1728]{2,1,0:T(8,128)(2,1)S(1)}, u32[]{:S(2)}, u32[]{:S(2)}) %collective-permute-start.52) | collective-permute-done | bytes 995360 | tf_op jit(solution)/shard_map/ppermute | solution.py:78
  328.4 12.0 %collective-permute-done.48 = bf16[2,144,1728]{2,1,0:T(8,128)(2,1)} collective-permute-done((bf16[2,144,1728]{2,1,0:T(8,128)(2,1)}, bf16[2,144,1728]{2,1,0:T(8,128)(2,1)}, u32[]{:S(2)}, u32[]{:S(2)}) %collective-permute-start.48) | collective-permute-done | bytes 995360 | tf_op jit(solution)/shard_map/ppermute | solution.py:78
  352.2 9.3 %attend_back.1 = (bf16[512,256]{1,0:T(8,128)(2,1)S(1)}, f32[512,1152]{1,0:T(8,128)}, bf16[2048,512]{1,0:T(8,128)(2,1)}, f32[1,256]{1,0:T(1,128)S(1)}) custom-call(bf16[512,1152]{1,0:T(8,128)(2,1)S(1)} %bitcast.410, bf16[512,256]{1,0:T(8,128)(2,1)S(1)} %copy-done.18, s32[512,1]{1,0:T(8,128)S(1)} %copy-done.10, s32[512,1]{1,0:T(8,128)S(1)} %copy-done.12, ...), custom_call_target="tpu_custom_call" | custom-call | flops 1 | bytes 1 | tf_op jit(solution)/shard_map/attend_back/pallas_call | solution.py:325
  380.9 16.4 %collective-permute-done.47 = bf16[2,144,1728]{2,1,0:T(8,128)(2,1)S(1)} collective-permute-done((bf16[2,144,1728]{2,1,0:T(8,128)(2,1)}, bf16[2,144,1728]{2,1,0:T(8,128)(2,1)S(1)}, u32[]{:S(2)}, u32[]{:S(2)}) %collective-permute-start.47) | collective-permute-done | bytes 995360 | tf_op jit(solution)/shard_map/ppermute | solution.py:139
  403.3 11.0 %collective-permute-done.49 = bf16[4,128,512]{2,1,0:T(8,128)(2,1)S(1)} collective-permute-done((bf16[4,128,512]{2,1,0:T(8,128)(2,1)S(1)}, bf16[4,128,512]{2,1,0:T(8,128)(2,1)S(1)}, u32[]{:S(2)}, u32[]{:S(2)}) %collective-permute-start.49) | collective-permute-done | bytes 524320 | tf_op jit(solution)/shard_map/ppermute | solution.py:78
  414.5 9.7 %collective-permute-done.50 = bf16[2,144,1728]{2,1,0:T(8,128)(2,1)S(1)} collective-permute-done((bf16[2,144,1728]{2,1,0:T(8,128)(2,1)S(1)}, bf16[2,144,1728]{2,1,0:T(8,128)(2,1)S(1)}, u32[]{:S(2)}, u32[]{:S(2)}) %collective-permute-start.50) | collective-permute-done | bytes 995360 | tf_op jit(solution)/shard_map/ppermute | solution.py:139
  466.0 15.6 %collective-permute-done.60 = bf16[288,256]{1,0:T(8,128)(2,1)S(1)} collective-permute-done((bf16[288,256]{1,0:T(8,128)(2,1)S(1)}, bf16[288,256]{1,0:T(8,128)(2,1)S(1)}, u32[]{:S(2)}, u32[]{:S(2)}) %collective-permute-start.60) | collective-permute-done | bytes 147488 | tf_op jit(solution)/shard_map/ppermute | solution.py:78
  483.4 5.2 %collective-permute-done.61 = bf16[288,256]{1,0:T(8,128)(2,1)S(1)} collective-permute-done((bf16[288,256]{1,0:T(8,128)(2,1)S(1)}, bf16[288,256]{1,0:T(8,128)(2,1)S(1)}, u32[]{:S(2)}, u32[]{:S(2)}) %collective-permute-start.61) | collective-permute-done | bytes 147488 | tf_op jit(solution)/shard_map/ppermute | solution.py:78
  (604 shorter events, 260.7 us)
Async XLA Ops:
  22.3 25.0 %collective-permute-start.4 = (bf16[2,144,1728]{2,1,0:T(8,128)(2,1)}, bf16[2,144,1728]{2,1,0:T(8,128)(2,1)}, u32[]{:S(2)}, u32[]{:S(2)}) collective-permute-start(bf16[2,144,1728]{2,1,0:T(8,128)(2,1)} %get-tuple-element.84), channel_id=1, source_target_pairs={{0,8},{8,24},{24,16},{16,0},{1,9},{9,25},{25,17},{17,1},{2,10},{10... | collective-permute-start | bytes 2985992 | tf_op jit(solution)/shard_map/ppermute | solution.py:139
  34.2 24.0 %collective-permute-start.8 = (bf16[2,144,1728]{2,1,0:T(8,128)(2,1)}, bf16[2,144,1728]{2,1,0:T(8,128)(2,1)S(1)}, u32[]{:S(2)}, u32[]{:S(2)}) collective-permute-start(bf16[2,144,1728]{2,1,0:T(8,128)(2,1)} %get-tuple-element.84), channel_id=1, source_target_pairs={{0,4},{4,0},{1,5},{5,1},{2,6},{6,2},{3,7},{7,3},{8,12},{12,8},{9,1... | collective-permute-start | bytes 2985992 | tf_op jit(solution)/shard_map/ppermute | solution.py:78
  49.0 23.9 %collective-permute-start.7 = (bf16[2,144,1728]{2,1,0:T(8,128)(2,1)}, bf16[2,144,1728]{2,1,0:T(8,128)(2,1)}, u32[]{:S(2)}, u32[]{:S(2)}) collective-permute-start(bf16[2,144,1728]{2,1,0:T(8,128)(2,1)} %collective-permute-done.4), channel_id=1, source_target_pairs={{0,8},{8,24},{24,16},{16,0},{1,9},{9,25},{25,17},{17,1},{2,10},{10... | collective-permute-start | bytes 2985992 | tf_op jit(solution)/shard_map/ppermute | solution.py:139
  58.2 25.5 %collective-permute-start.10 = (bf16[2,144,1728]{2,1,0:T(8,128)(2,1)}, bf16[2,144,1728]{2,1,0:T(8,128)(2,1)}, u32[]{:S(2)}, u32[]{:S(2)}) collective-permute-start(bf16[2,144,1728]{2,1,0:T(8,128)(2,1)} %collective-permute-done.4), channel_id=1, source_target_pairs={{0,4},{4,0},{1,5},{5,1},{2,6},{6,2},{3,7},{7,3},{8,12},{12,8},{9,1... | collective-permute-start | bytes 2985992 | tf_op jit(solution)/shard_map/ppermute | solution.py:78
  72.8 22.9 %collective-permute-start.9 = (bf16[2,144,1728]{2,1,0:T(8,128)(2,1)}, bf16[2,144,1728]{2,1,0:T(8,128)(2,1)}, u32[]{:S(2)}, u32[]{:S(2)}) collective-permute-start(bf16[2,144,1728]{2,1,0:T(8,128)(2,1)} %collective-permute-done.7), channel_id=1, source_target_pairs={{0,8},{8,24},{24,16},{16,0},{1,9},{9,25},{25,17},{17,1},{2,10},{10... | collective-permute-start | bytes 2985992 | tf_op jit(solution)/shard_map/ppermute | solution.py:139
  121.8 22.8 %collective-permute-start.22 = (bf16[2,144,1728]{2,1,0:T(8,128)(2,1)}, bf16[2,144,1728]{2,1,0:T(8,128)(2,1)S(1)}, u32[]{:S(2)}, u32[]{:S(2)}) collective-permute-start(bf16[2,144,1728]{2,1,0:T(8,128)(2,1)} %collective-permute-done.7), channel_id=1, source_target_pairs={{0,4},{4,0},{1,5},{5,1},{2,6},{6,2},{3,7},{7,3},{8,12},{12,8},{9,1... | collective-permute-start | bytes 2985992 | tf_op jit(solution)/shard_map/ppermute | solution.py:78
  159.0 23.1 %collective-permute-start.29 = (bf16[2,144,1728]{2,1,0:T(8,128)(2,1)S(1)}, bf16[2,144,1728]{2,1,0:T(8,128)(2,1)S(1)}, u32[]{:S(2)}, u32[]{:S(2)}) collective-permute-start(bf16[2,144,1728]{2,1,0:T(8,128)(2,1)S(1)} %collective-permute-done.25), channel_id=1, source_target_pairs={{0,8},{8,24},{24,16},{16,0},{1,9},{9,25},{25,17},{17,1},{2,10},{10... | collective-permute-start | bytes 2985992 | tf_op jit(solution)/shard_map/ppermute | solution.py:139
  245.6 29.4 %collective-permute-start.34 = (bf16[2,144,1728]{2,1,0:T(8,128)(2,1)}, bf16[2,144,1728]{2,1,0:T(8,128)(2,1)S(1)}, u32[]{:S(2)}, u32[]{:S(2)}) collective-permute-start(bf16[2,144,1728]{2,1,0:T(8,128)(2,1)} %dynamic-slice_bitcast_fusion), channel_id=1, source_target_pairs={{0,8},{8,24},{24,16},{16,0},{1,9},{9,25},{25,17},{17,1},{2,10},{10... | collective-permute-start | bytes 2985992 | tf_op jit(solution)/shard_map/ppermute | solution.py:139
  270.8 25.7 %collective-permute-start.43 = (bf16[2,144,1728]{2,1,0:T(8,128)(2,1)S(1)}, bf16[2,144,1728]{2,1,0:T(8,128)(2,1)S(1)}, u32[]{:S(2)}, u32[]{:S(2)}) collective-permute-start(bf16[2,144,1728]{2,1,0:T(8,128)(2,1)S(1)} %pad_maximum_fusion.4), channel_id=1, source_target_pairs={{0,4},{4,0},{1,5},{5,1},{2,6},{6,2},{3,7},{7,3},{8,12},{12,8},{9,1... | collective-permute-start | bytes 2985992 | tf_op jit(solution)/shard_map/ppermute | solution.py:78
  272.5 46.1 %collective-permute-start.52 = (bf16[2,144,1728]{2,1,0:T(8,128)(2,1)S(1)}, bf16[2,144,1728]{2,1,0:T(8,128)(2,1)S(1)}, u32[]{:S(2)}, u32[]{:S(2)}) collective-permute-start(bf16[2,144,1728]{2,1,0:T(8,128)(2,1)S(1)} %pad_maximum_fusion.6), channel_id=1, source_target_pairs={{0,4},{4,0},{1,5},{5,1},{2,6},{6,2},{3,7},{7,3},{8,12},{12,8},{9,1... | collective-permute-start | bytes 2985992 | tf_op jit(solution)/shard_map/ppermute | solution.py:78
  275.1 24.3 %collective-permute-start.35 = (bf16[2,128,1152]{2,1,0:T(8,128)(2,1)S(1)}, bf16[2,128,1152]{2,1,0:T(8,128)(2,1)S(1)}, u32[]{:S(2)}, u32[]{:S(2)}) collective-permute-start(bf16[2,128,1152]{2,1,0:T(8,128)(2,1)S(1)} %fusion.17), channel_id=1, source_target_pairs={{0,1},{1,0},{2,3},{3,2},{4,5},{5,4},{6,7},{7,6},{8,9},{9,8},{10,11... | collective-permute-start | bytes 1769480 | tf_op jit(solution)/shard_map/ppermute | solution.py:78
  275.5 43.2 %collective-permute-start.37 = (bf16[2,144,1728]{2,1,0:T(8,128)(2,1)S(1)}, bf16[2,144,1728]{2,1,0:T(8,128)(2,1)S(1)}, u32[]{:S(2)}, u32[]{:S(2)}) collective-permute-start(bf16[2,144,1728]{2,1,0:T(8,128)(2,1)S(1)} %fusion.4), channel_id=1, source_target_pairs={{0,8},{8,24},{24,16},{16,0},{1,9},{9,25},{25,17},{17,1},{2,10},{10... | collective-permute-start | bytes 2985992 | tf_op jit(solution)/shard_map/ppermute | solution.py:139
  297.7 42.7 %collective-permute-start.48 = (bf16[2,144,1728]{2,1,0:T(8,128)(2,1)}, bf16[2,144,1728]{2,1,0:T(8,128)(2,1)}, u32[]{:S(2)}, u32[]{:S(2)}) collective-permute-start(bf16[2,144,1728]{2,1,0:T(8,128)(2,1)} %pad_maximum_fusion.5), channel_id=1, source_target_pairs={{0,4},{4,0},{1,5},{5,1},{2,6},{6,2},{3,7},{7,3},{8,12},{12,8},{9,1... | collective-permute-start | bytes 2985992 | tf_op jit(solution)/shard_map/ppermute | solution.py:78
  326.2 24.6 %collective-permute-start.42 = (bf16[2,144,1728]{2,1,0:T(8,128)(2,1)S(1)}, bf16[2,144,1728]{2,1,0:T(8,128)(2,1)S(1)}, u32[]{:S(2)}, u32[]{:S(2)}) collective-permute-start(bf16[2,144,1728]{2,1,0:T(8,128)(2,1)S(1)} %fusion.3), channel_id=1, source_target_pairs={{0,8},{8,24},{24,16},{16,0},{1,9},{9,25},{25,17},{17,1},{2,10},{10... | collective-permute-start | bytes 2985992 | tf_op jit(solution)/shard_map/ppermute | solution.py:139
  340.4 89.0 %collective-permute-start.51 = (bf16[2,144,1728]{2,1,0:T(8,128)(2,1)}, bf16[2,144,1728]{2,1,0:T(8,128)(2,1)}, u32[]{:S(2)}, u32[]{:S(2)}) collective-permute-start(bf16[2,144,1728]{2,1,0:T(8,128)(2,1)} %pad_maximum_fusion.7), channel_id=1, source_target_pairs={{0,4},{4,0},{1,5},{5,1},{2,6},{6,2},{3,7},{7,3},{8,12},{12,8},{9,1... | collective-permute-start | bytes 2985992 | tf_op jit(solution)/shard_map/ppermute | solution.py:78
  371.0 30.2 %collective-permute-start.44 = (bf16[2,128,1152]{2,1,0:T(8,128)(2,1)S(1)}, bf16[2,128,1152]{2,1,0:T(8,128)(2,1)S(1)}, u32[]{:S(2)}, u32[]{:S(2)}) collective-permute-start(bf16[2,128,1152]{2,1,0:T(8,128)(2,1)S(1)} %fusion.18), channel_id=1, source_target_pairs={{0,1},{1,0},{2,3},{3,2},{4,5},{5,4},{6,7},{7,6},{8,9},{9,8},{10,11... | collective-permute-start | bytes 1769480 | tf_op jit(solution)/shard_map/ppermute | solution.py:78
  371.0 26.3 %collective-permute-start.47 = (bf16[2,144,1728]{2,1,0:T(8,128)(2,1)}, bf16[2,144,1728]{2,1,0:T(8,128)(2,1)S(1)}, u32[]{:S(2)}, u32[]{:S(2)}) collective-permute-start(bf16[2,144,1728]{2,1,0:T(8,128)(2,1)} %convert_add_fusion.8), channel_id=1, source_target_pairs={{0,8},{8,24},{24,16},{16,0},{1,9},{9,25},{25,17},{17,1},{2,10},{10... | collective-permute-start | bytes 2985992 | tf_op jit(solution)/shard_map/ppermute | solution.py:139
  372.5 26.5 %collective-permute-start.46 = (bf16[2,4,128,512]{3,2,1,0:T(8,128)(2,1)S(1)}, bf16[2,4,128,512]{3,2,1,0:T(8,128)(2,1)S(1)}, u32[]{:S(2)}, u32[]{:S(2)}) collective-permute-start(bf16[2,4,128,512]{3,2,1,0:T(8,128)(2,1)S(1)} %bitcast.428), channel_id=1, source_target_pairs={{0,1},{1,0},{2,3},{3,2},{4,5},{5,4},{6,7},{7,6},{8,9},{9,8},{10,11... | collective-permute-start | bytes 3145736 | tf_op jit(solution)/shard_map/ppermute | solution.py:78
  399.0 25.3 %collective-permute-start.50 = (bf16[2,144,1728]{2,1,0:T(8,128)(2,1)S(1)}, bf16[2,144,1728]{2,1,0:T(8,128)(2,1)S(1)}, u32[]{:S(2)}, u32[]{:S(2)}) collective-permute-start(bf16[2,144,1728]{2,1,0:T(8,128)(2,1)S(1)} %add_convert_fusion), channel_id=1, source_target_pairs={{0,8},{8,24},{24,16},{16,0},{1,9},{9,25},{25,17},{17,1},{2,10},{10... | collective-permute-start | bytes 2985992 | tf_op jit(solution)/shard_map/ppermute | solution.py:139
  402.1 36.8 %collective-permute-start.45 = (bf16[128,1152]{1,0:T(8,128)(2,1)}, bf16[128,1152]{1,0:T(8,128)(2,1)}, u32[]{:S(2)}, u32[]{:S(2)}) collective-permute-start(bf16[128,1152]{1,0:T(8,128)(2,1)} %fusion.31), channel_id=1, source_target_pairs={{0,2},{2,0},{1,3},{3,1},{4,6},{6,4},{5,7},{7,5},{8,10},{10,8},{9,1... | collective-permute-start | bytes 884744 | tf_op jit(solution)/shard_map/ppermute | solution.py:78
  429.4 29.5 %collective-permute-start.59 = (bf16[4,288,256]{2,1,0:T(8,128)(2,1)}, bf16[4,288,256]{2,1,0:T(8,128)(2,1)}, u32[]{:S(2)}, u32[]{:S(2)}) collective-permute-start(bf16[4,288,256]{2,1,0:T(8,128)(2,1)} %dynamic-slice_bitcast_fusion.1), channel_id=1, source_target_pairs={{0,4},{4,0},{1,5},{5,1},{2,6},{6,2},{3,7},{7,3},{8,12},{12,8},{9,1... | collective-permute-start | bytes 1769480 | tf_op jit(solution)/shard_map/ppermute | solution.py:78
  449.7 40.9 %collective-permute-start.67 = (bf16[2,144,1728]{2,1,0:T(8,128)(2,1)S(1)}, bf16[2,144,1728]{2,1,0:T(8,128)(2,1)S(1)}, u32[]{:S(2)}, u32[]{:S(2)}) collective-permute-start(bf16[2,144,1728]{2,1,0:T(8,128)(2,1)S(1)} %copy-done.78), channel_id=1, source_target_pairs={{0,8},{8,24},{24,16},{16,0},{1,9},{9,25},{25,17},{17,1},{2,10},{10... | collective-permute-start | bytes 2985992 | tf_op jit(solution)/shard_map/ppermute | solution.py:139
  457.6 32.8 %collective-permute-start.57 = (bf16[2,128,1152]{2,1,0:T(8,128)(2,1)S(1)}, bf16[2,128,1152]{2,1,0:T(8,128)(2,1)S(1)}, u32[]{:S(2)}, u32[]{:S(2)}) collective-permute-start(bf16[2,128,1152]{2,1,0:T(8,128)(2,1)S(1)} %pad_maximum_fusion.17), channel_id=1, source_target_pairs={{0,1},{1,0},{2,3},{3,2},{4,5},{5,4},{6,7},{7,6},{8,9},{9,8},{10,11... | collective-permute-start | bytes 1769480 | tf_op jit(solution)/shard_map/ppermute | solution.py:78
  464.7 23.9 %collective-permute-start.61 = (bf16[288,256]{1,0:T(8,128)(2,1)S(1)}, bf16[288,256]{1,0:T(8,128)(2,1)S(1)}, u32[]{:S(2)}, u32[]{:S(2)}) collective-permute-start(bf16[288,256]{1,0:T(8,128)(2,1)S(1)} %get-tuple-element.215), channel_id=1, source_target_pairs={{0,16},{8,24},{16,0},{24,8},{1,17},{9,25},{17,1},{25,9},{2,18},{10... | collective-permute-start | bytes 442376 | tf_op jit(solution)/shard_map/ppermute | solution.py:78
  (168 other events, 2114.3 us)
